TPU v7x, 128 devices: a whole 4x4x4 slice. The times are simulated.
128 devices in a mesh: wide: 8 (over y, core), col: 16 (over z, x).
Axes of the slice: x: 4, y: 4, z: 4, core: 2. Of those that a mesh axis runs over, the one named last changes fastest.
Arguments:
- rhs: float32 [98304, 256], P(('wide', 'col')), may hold values from -6 to 6
- basis: bfloat16 [98304, 256], P(('wide', 'col')), may hold values from -0.21875 to 0.21875
- self_block: bfloat16 [98304, 768], P(('wide', 'col'))
- near_block: bfloat16 [128, 8, 768, 768], P(('wide', 'col')), may hold values from -0.0546875 to 0.0546875
- near_ids: int32 [128, 8], P(('wide', 'col')), may hold values from -1 to 127, as said below
- couplings: bfloat16 [128, 40, 256, 256], P(('wide', 'col')), may hold values from -0.09375 to 0.09375
- far_ids: int32 [128, 40], P(('wide', 'col')), may hold values from -1 to 127, as said below
- intersection_start: int32 [128, 2], P(('wide', 'col')), may hold values from 0 to 512
- schwarz_inverse: bfloat16 [128, 1280, 1280], P(('wide', 'col'))
Outputs:
- solution: float32 [98304, 256], P(('wide', 'col'))
Inputs may be any that keep to these rules, and one draw needn't show every extreme that they name: `near_ids`: row c lists every cluster adjacent to cluster c on the grid (larger index distance 1; id = first index * 16 + second), ids first and -1 after them; rows of corner and edge clusters end in -1. `far_ids`: row c lists distinct clusters whose larger grid index distance from cluster c is 2 to 3, ids first and -1 after them; counts are ragged, and some rows list every such cluster. `intersection_start`: column 0 starts the rows taken by the domain of the cluster before along the second grid index, column 1 those taken by the one after.
All inputs are finite; a program needn't handle non-finite values.
Results may differ from a plain program's by a relative error of at most 0.0025.
The roundings to bfloat16 on the way count: a program that leaves them out, or rounds other values in their place, can miss the bound.
Values may be sent and summed in bfloat16 or wider, within the bound.
A program may use at most 128 MiB of HBM per device.

v0:
```python
import jax
import jax.numpy as jnp
from jax import lax
from jax.sharding import PartitionSpec as P

REACH = 3
ITERS = 2


HIGHEST_PREC = lax.Precision.HIGHEST
GROUP_SLOTS = 8


def passed_along(block, axis, distance):
    devices = range(lax.axis_size(axis))
    route = [(i - distance, i) for i in devices if i - distance in devices]
    return lax.ppermute(block, axis, route)


def with_halo(block, sides, width):
    for axis, dim in sides:
        count = lax.axis_size(axis)
        forward = [(i, i + 1) for i in range(count - 1)]
        backward = [(target, source) for source, target in forward]
        low = lax.ppermute(
            lax.slice_in_dim(block, block.shape[dim] - width, None, axis=dim), axis, forward
        )
        high = lax.ppermute(lax.slice_in_dim(block, 0, width, axis=dim), axis, backward)
        block = jnp.concatenate([low, block, high], axis=dim)
    return block


def local_gram(left, right):
    return lax.dot_general(
        left,
        right,
        (((0,), (0,)), ((), ())),
        precision=HIGHEST_PREC,
        preferred_element_type=jnp.float32,
    )


def lower_solve(factor, matrix):
    return lax.linalg.triangular_solve(
        factor, matrix, left_side=False, lower=True, transpose_a=True
    )


def far_window(coefficients):
    strip_row = jnp.stack(
        [
            coefficients if offset == 0 else passed_along(coefficients, "col", -offset)
            for offset in range(-REACH, REACH + 1)
        ]
    )
    window = jnp.stack(
        [
            strip_row if offset == 0 else passed_along(strip_row, "wide", -offset)
            for offset in range(-REACH, REACH + 1)
        ]
    )
    return window


def operate(vector_in, basis, self_block, near_block, near_ids, couplings, far_ids):
    rounded = vector_in.astype(jnp.bfloat16)
    cluster_rows, width = rounded.shape
    rank = basis.shape[1]
    wide_pos = lax.axis_index("wide")
    col_pos = lax.axis_index("col")
    col_count = lax.axis_size("col")
    result = jnp.dot(self_block, rounded, preferred_element_type=jnp.float32)
    beside_all = with_halo(rounded[None, None], (("wide", 0), ("col", 1)), 1)
    for slot_index in range(near_ids.shape[1]):
        neighbour = near_ids[0, slot_index]
        safe_id = jnp.maximum(neighbour, 0)
        wide_off = safe_id // col_count - wide_pos + 1
        col_off = safe_id % col_count - col_pos + 1
        other = lax.dynamic_slice(
            beside_all, (wide_off, col_off, 0, 0), (1, 1, cluster_rows, width)
        )[0, 0]
        product = jnp.dot(near_block[0, slot_index], other, preferred_element_type=jnp.float32)
        result = result + jnp.where(neighbour >= 0, product, jnp.zeros_like(product))
    coefficients = lax.dot_general(
        basis, rounded, (((0,), (0,)), ((), ())), preferred_element_type=jnp.float32
    ).astype(jnp.bfloat16)
    window = far_window(coefficients)
    span = 2 * REACH + 1
    flat_window = window.reshape(span * span, rank, width)
    far_list = far_ids[0]
    live_count = jnp.sum((far_list >= 0).astype(jnp.int32))
    group_count = (live_count + GROUP_SLOTS - 1) // GROUP_SLOTS

    def add_group(group_index, running):
        first_slot = group_index * GROUP_SLOTS
        targets = lax.dynamic_slice_in_dim(far_list, first_slot, GROUP_SLOTS, 0)
        safe_ids = jnp.maximum(targets, 0)
        flat_index = (safe_ids // col_count - wide_pos + REACH) * span + (
            safe_ids % col_count - col_pos + REACH
        )
        pieces_in = jnp.take(flat_window, flat_index, axis=0)
        coupling_group = lax.dynamic_slice_in_dim(couplings[0], first_slot, GROUP_SLOTS, 0)
        live_slots = (targets >= 0)[:, None, None]
        coupling_group = jnp.where(live_slots, coupling_group, jnp.zeros_like(coupling_group))
        return running + jnp.einsum(
            "lrs,lsk->rk", coupling_group, pieces_in, preferred_element_type=jnp.float32
        )

    far_sum = lax.fori_loop(0, group_count, add_group, jnp.zeros((rank, width), jnp.float32))
    return result + jnp.dot(basis, far_sum.astype(jnp.bfloat16), preferred_element_type=jnp.float32)


def add_rows(matrix, addend, start):
    current = lax.dynamic_slice_in_dim(matrix, start, addend.shape[0], 0)
    return lax.dynamic_update_slice_in_dim(matrix, current + addend, start, 0)


def precondition(vector_in, intersection_start, schwarz_inverse):
    rounded = vector_in.astype(jnp.bfloat16)
    cluster_rows = rounded.shape[0]
    margin = (schwarz_inverse.shape[1] - cluster_rows) // 2
    starts = intersection_start[0]
    prev_whole, prev_starts = passed_along((rounded, intersection_start), "col", 1)
    next_whole, next_starts = passed_along((rounded, intersection_start), "col", -1)
    prev_rows = lax.dynamic_slice_in_dim(prev_whole, prev_starts[0, 1], margin, 0)
    next_rows = lax.dynamic_slice_in_dim(next_whole, next_starts[0, 0], margin, 0)
    domain = jnp.concatenate([prev_rows, rounded, next_rows], axis=0)
    solved = jnp.dot(schwarz_inverse[0], domain, preferred_element_type=jnp.float32)
    result = solved[margin : margin + cluster_rows]
    from_next = passed_along(solved[:margin], "col", -1)
    from_prev = passed_along(solved[margin + cluster_rows :], "col", 1)
    result = add_rows(result, from_next, starts[1])
    result = add_rows(result, from_prev, starts[0])
    return result


def on_device(
    rhs,
    basis,
    self_block,
    near_block,
    near_ids,
    couplings,
    far_ids,
    intersection_start,
    schwarz_inverse,
):
    width = rhs.shape[1]
    first_sum = lax.psum(local_gram(rhs, rhs), ("wide", "col"))
    factor = jnp.linalg.cholesky(first_sum)
    beta_block = factor.T
    bases = [lower_solve(factor, rhs)]
    directions = []
    columns = []
    for iteration in range(ITERS):
        precond_out = precondition(bases[-1], intersection_start, schwarz_inverse)
        image = operate(precond_out, basis, self_block, near_block, near_ids, couplings, far_ids)
        stacked = jnp.concatenate(bases, axis=1)
        projected = lax.psum(local_gram(stacked, image), ("wide", "col"))
        image = image - jnp.dot(stacked, projected, precision=HIGHEST_PREC)
        gram_sum = lax.psum(local_gram(image, image), ("wide", "col"))
        factor = jnp.linalg.cholesky(gram_sum)
        columns.append((projected, factor.T))
        directions.append(precond_out)
        if iteration + 1 < ITERS:
            bases.append(lower_solve(factor, image))
    hessen = jnp.zeros(((ITERS + 1) * width, ITERS * width), jnp.float32)
    for column_index, (projected, sub_block) in enumerate(columns):
        upper_rows = (column_index + 1) * width
        hessen = hessen.at[:upper_rows, column_index * width : (column_index + 1) * width].set(
            projected
        )
        hessen = hessen.at[
            upper_rows : upper_rows + width, column_index * width : (column_index + 1) * width
        ].set(sub_block)
    normal_matrix = jnp.dot(hessen.T, hessen, precision=HIGHEST_PREC)
    target = jnp.dot(hessen[:width].T, beta_block, precision=HIGHEST_PREC)
    small_factor = jnp.linalg.cholesky(normal_matrix)
    middle = lax.linalg.triangular_solve(small_factor, target, left_side=True, lower=True)
    weights_y = lax.linalg.triangular_solve(
        small_factor, middle, left_side=True, lower=True, transpose_a=True
    )
    return jnp.dot(jnp.concatenate(directions, axis=1), weights_y, precision=HIGHEST_PREC)


def solution(mesh):
    in_specs = (
        P(("wide", "col"), None),
        P(("wide", "col"), None),
        P(("wide", "col"), None),
        P(("wide", "col"), None, None, None),
        P(("wide", "col"), None),
        P(("wide", "col"), None, None, None),
        P(("wide", "col"), None),
        P(("wide", "col"), None),
        P(("wide", "col"), None, None),
    )
    out_specs = P(("wide", "col"), None)
    return jax.shard_map(
        on_device, mesh=mesh, in_specs=in_specs, out_specs=out_specs, check_vma=False
    )
```

profile of v0, /device:TPU:1, one launch (start us, length us, event | category | flops | bytes accessed | tf_op | source)
XLA Modules:
  0.0 1555.5 jit_solution(12817224653365156530)
XLA Ops:
  10.3 146.7 %all-reduce.9.cloned.1.call-done = f32[256,256]{0,1:T(8,128)} async-done(((f32[256,256]{0,1:T(8,128)}), f32[256,256]{0,1:T(8,128)}) %all-reduce.9.cloned.1.call-update) | async-done | bytes 262160 | tf_op jit(solution)/shard_map/psum | solution.py:149
  159.7 11.7 cholesky.392
  172.1 10.4 custom-call.47
  186.2 13.2 cholesky.402
  211.1 21.1 %custom-call.48 = f32[2,128,128]{1,2,0:T(8,128)} custom-call(f32[2,128,128]{2,1,0:T(8,128)} %get-tuple-element.295), custom_call_target="InvertDiagBlocksLowerTriangular" | custom-call | tf_op jit(solution)/shard_map/triangular_solve/custom-call.9 | solution.py:44
  339.1 19.1 %collective-permute-done.6 = bf16[1,1,768,256]{2,3,1,0:T(8,128)(2,1)} collective-permute-done((bf16[1,1,768,256]{2,3,1,0:T(8,128)(2,1)}, bf16[1,1,768,256]{2,3,1,0:T(8,128)(2,1)}, u32[]{:S(2)}, u32[]{:S(2)}) %collective-permute-start.6) | collective-permute-done | bytes 393248 | tf_op jit(solution)/shard_map/ppermute | solution.py:25
  421.3 192.6 %all-reduce.11.cloned.1.call-done = f32[256,256]{1,0:T(8,128)} async-done(((f32[256,256]{1,0:T(8,128)}), f32[256,256]{1,0:T(8,128)}) %all-reduce.11.cloned.1.call-update) | async-done | bytes 262160 | tf_op jit(solution)/shard_map/psum | solution.py:159
  618.9 138.9 %all-reduce.13.cloned.1.call-done = f32[256,256]{0,1:T(8,128)} async-done(((f32[256,256]{0,1:T(8,128)}), f32[256,256]{0,1:T(8,128)}) %all-reduce.13.cloned.1.call-update) | async-done | bytes 262160 | tf_op jit(solution)/shard_map/psum | solution.py:161
  762.0 13.2 cholesky.419
  778.2 11.3 custom-call.49
  792.9 13.2 cholesky.429
  820.2 21.1 %custom-call.50 = f32[2,128,128]{1,2,0:T(8,128)} custom-call(f32[2,128,128]{2,1,0:T(8,128)} %get-tuple-element.296), custom_call_target="InvertDiagBlocksLowerTriangular" | custom-call | tf_op jit(solution)/shard_map/triangular_solve/custom-call.9 | solution.py:44
  922.5 31.3 %collective-permute-done.26 = bf16[1,1,768,256]{2,3,1,0:T(8,128)(2,1)S(1)} collective-permute-done((bf16[1,1,768,256]{2,3,1,0:T(8,128)(2,1)S(1)}, bf16[1,1,768,256]{2,3,1,0:T(8,128)(2,1)S(1)}, u32[]{:S(2)}, u32[]{:S(2)}) %collective-permute-start.26) | collective-permute-done | bytes 393248 | tf_op jit(solution)/shard_map/ppermute | solution.py:25
  1017.5 189.2 %all-reduce.15.cloned.1.call-done = f32[512,256]{1,0:T(8,128)} async-done(((f32[512,256]{1,0:T(8,128)}), f32[512,256]{1,0:T(8,128)}) %all-reduce.15.cloned.1.call-update) | async-done | bytes 524304 | tf_op jit(solution)/shard_map/psum | solution.py:159
  1220.9 131.3 %all-reduce.17.cloned.1.call-done = f32[256,256]{0,1:T(8,128)} async-done(((f32[256,256]{0,1:T(8,128)}), f32[256,256]{0,1:T(8,128)}) %all-reduce.17.cloned.1.call-update) | async-done | bytes 262160 | tf_op jit(solution)/shard_map/psum | solution.py:161
  1354.3 11.7 cholesky.446
  1376.4 11.7 cholesky.456
  1396.8 11.7 cholesky.167
  1408.7 9.8 custom-call.37
  1421.0 11.9 cholesky.190
  1445.7 11.7 cholesky.294
  1469.4 11.9 cholesky.307
  1484.7 10.6 while.35
  1495.3 40.2 %custom-call.39 = f32[4,128,128]{1,2,0:T(8,128)S(1)} custom-call(f32[4,128,128]{2,1,0:T(8,128)} %get-tuple-element.288), custom_call_target="InvertDiagBlocksLowerTriangular" | custom-call | tf_op jit(solution)/shard_map/triangular_solve | solution.py:180
  (407 shorter events, 460.3 us)
Async XLA Ops:
  6.5 150.4 %all-reduce.9.cloned.1.call-start = ((), (), s32[]{:S(2)}) async-start(), calls=%async_computation | async-start | bytes 524288 | tf_op jit(solution)/shard_map/psum | solution.py:149
  10.2 603.7 %all-reduce.11.cloned.1.call-start = ((), (), s32[]{:S(2)}) async-start(), calls=%async_computation.1 | async-start | bytes 524288 | tf_op jit(solution)/shard_map/psum | solution.py:159
  308.1 55.7 %collective-permute-start.16 = (bf16[7,256,256]{1,2,0:T(8,128)(2,1)}, bf16[7,256,256]{1,2,0:T(8,128)(2,1)}, u32[]{:S(2)}, u32[]{:S(2)}) collective-permute-start(bf16[7,256,256]{1,2,0:T(8,128)(2,1)} %bitcast_dynamic-update-slice_fusion.25), channel_id=1, source_target_pairs={{0,48},{16,64},{32,80},{48,96},{64,112},{1,49},{17,65},{33,81},{49... | collective-permute-start | bytes 2752520 | tf_op jit(solution)/shard_map/ppermute | solution.py:17
  316.5 50.8 %collective-permute-start.17 = (bf16[7,256,256]{1,2,0:T(8,128)(2,1)}, bf16[7,256,256]{1,2,0:T(8,128)(2,1)}, u32[]{:S(2)}, u32[]{:S(2)}) collective-permute-start(bf16[7,256,256]{1,2,0:T(8,128)(2,1)} %bitcast_dynamic-update-slice_fusion.25), channel_id=1, source_target_pairs={{0,32},{16,48},{32,64},{48,80},{64,96},{80,112},{1,33},{17,49},{33... | collective-permute-start | bytes 2752520 | tf_op jit(solution)/shard_map/ppermute | solution.py:17
  319.5 38.7 %collective-permute-start.6 = (bf16[1,1,768,256]{2,3,1,0:T(8,128)(2,1)}, bf16[1,1,768,256]{2,3,1,0:T(8,128)(2,1)}, u32[]{:S(2)}, u32[]{:S(2)}) collective-permute-start(bf16[1,1,768,256]{2,3,1,0:T(8,128)(2,1)} %convert_bitcast_fusion.1), channel_id=1, source_target_pairs={{0,16},{16,32},{32,48},{48,64},{64,80},{80,96},{96,112},{1,17},{17... | collective-permute-start | bytes 1179656 | tf_op jit(solution)/shard_map/ppermute | solution.py:25
  321.5 38.7 %collective-permute-start.7 = (bf16[1,1,768,256]{2,3,1,0:T(8,128)(2,1)}, bf16[1,1,768,256]{2,3,1,0:T(8,128)(2,1)}, u32[]{:S(2)}, u32[]{:S(2)}) collective-permute-start(bf16[1,1,768,256]{2,3,1,0:T(8,128)(2,1)} %convert_bitcast_fusion.1), channel_id=1, source_target_pairs={{16,0},{32,16},{48,32},{64,48},{80,64},{96,80},{112,96},{17,1},{33... | collective-permute-start | bytes 1179656 | tf_op jit(solution)/shard_map/ppermute | solution.py:28
  324.6 49.9 %collective-permute-start.18 = (bf16[7,256,256]{1,2,0:T(8,128)(2,1)}, bf16[7,256,256]{1,2,0:T(8,128)(2,1)}, u32[]{:S(2)}, u32[]{:S(2)}) collective-permute-start(bf16[7,256,256]{1,2,0:T(8,128)(2,1)} %bitcast_dynamic-update-slice_fusion.25), channel_id=1, source_target_pairs={{0,16},{16,32},{32,48},{48,64},{64,80},{80,96},{96,112},{1,17},{17... | collective-permute-start | bytes 2752520 | tf_op jit(solution)/shard_map/ppermute | solution.py:17
  358.2 23.7 %collective-permute-start.19 = (bf16[7,256,256]{1,2,0:T(8,128)(2,1)}, bf16[7,256,256]{1,2,0:T(8,128)(2,1)S(1)}, u32[]{:S(2)}, u32[]{:S(2)}) collective-permute-start(bf16[7,256,256]{1,2,0:T(8,128)(2,1)} %bitcast_dynamic-update-slice_fusion.25), channel_id=1, source_target_pairs={{16,0},{32,16},{48,32},{64,48},{80,64},{96,80},{112,96},{17,1},{33... | collective-permute-start | bytes 2752520 | tf_op jit(solution)/shard_map/ppermute | solution.py:17
  360.2 25.7 %collective-permute-start.20 = (bf16[7,256,256]{1,2,0:T(8,128)(2,1)}, bf16[7,256,256]{1,2,0:T(8,128)(2,1)S(1)}, u32[]{:S(2)}, u32[]{:S(2)}) collective-permute-start(bf16[7,256,256]{1,2,0:T(8,128)(2,1)} %bitcast_dynamic-update-slice_fusion.25), channel_id=1, source_target_pairs={{32,0},{48,16},{64,32},{80,48},{96,64},{112,80},{33,1},{49,17},{65... | collective-permute-start | bytes 2752520 | tf_op jit(solution)/shard_map/ppermute | solution.py:17
  367.3 38.0 %collective-permute-start.8 = (bf16[3,1,768,256]{2,3,1,0:T(8,128)(2,1)}, bf16[3,1,768,256]{2,3,1,0:T(8,128)(2,1)}, u32[]{:S(2)}, u32[]{:S(2)}) collective-permute-start(bf16[3,1,768,256]{2,3,1,0:T(8,128)(2,1)} %pad_maximum_fusion.2), channel_id=1, source_target_pairs={{0,1},{1,2},{2,3},{3,4},{4,5},{5,6},{6,7},{7,8},{8,9},{9,10},{10,1... | collective-permute-start | bytes 3538952 | tf_op jit(solution)/shard_map/ppermute | solution.py:25
  374.5 30.8 %collective-permute-start.9 = (bf16[3,1,768,256]{2,3,1,0:T(8,128)(2,1)}, bf16[3,1,768,256]{2,3,1,0:T(8,128)(2,1)}, u32[]{:S(2)}, u32[]{:S(2)}) collective-permute-start(bf16[3,1,768,256]{2,3,1,0:T(8,128)(2,1)} %pad_maximum_fusion.2), channel_id=1, source_target_pairs={{1,0},{2,1},{3,2},{4,3},{5,4},{6,5},{7,6},{8,7},{9,8},{10,9},{11,1... | collective-permute-start | bytes 3538952 | tf_op jit(solution)/shard_map/ppermute | solution.py:28
  421.2 336.6 %all-reduce.13.cloned.1.call-start = ((), (), s32[]{:S(2)}) async-start(), calls=%async_computation.2 | async-start | bytes 524288 | tf_op jit(solution)/shard_map/psum | solution.py:161
  618.7 588.1 %all-reduce.15.cloned.1.call-start = ((), (), s32[]{:S(2)}) async-start(), calls=%async_computation.3 | async-start | bytes 1048576 | tf_op jit(solution)/shard_map/psum | solution.py:159
  905.1 53.0 %collective-permute-start.36 = (bf16[7,256,256]{1,2,0:T(8,128)(2,1)}, bf16[7,256,256]{1,2,0:T(8,128)(2,1)}, u32[]{:S(2)}, u32[]{:S(2)}) collective-permute-start(bf16[7,256,256]{1,2,0:T(8,128)(2,1)} %bitcast_dynamic-update-slice_fusion.19), channel_id=1, source_target_pairs={{0,48},{16,64},{32,80},{48,96},{64,112},{1,49},{17,65},{33,81},{49... | collective-permute-start | bytes 2752520 | tf_op jit(solution)/shard_map/ppermute | solution.py:17
  912.7 48.9 %collective-permute-start.37 = (bf16[7,256,256]{1,2,0:T(8,128)(2,1)}, bf16[7,256,256]{1,2,0:T(8,128)(2,1)}, u32[]{:S(2)}, u32[]{:S(2)}) collective-permute-start(bf16[7,256,256]{1,2,0:T(8,128)(2,1)} %bitcast_dynamic-update-slice_fusion.19), channel_id=1, source_target_pairs={{0,32},{16,48},{32,64},{48,80},{64,96},{80,112},{1,33},{17,49},{33... | collective-permute-start | bytes 2752520 | tf_op jit(solution)/shard_map/ppermute | solution.py:17
  915.0 38.8 %collective-permute-start.26 = (bf16[1,1,768,256]{2,3,1,0:T(8,128)(2,1)S(1)}, bf16[1,1,768,256]{2,3,1,0:T(8,128)(2,1)S(1)}, u32[]{:S(2)}, u32[]{:S(2)}) collective-permute-start(bf16[1,1,768,256]{2,3,1,0:T(8,128)(2,1)S(1)} %convert_bitcast_fusion), channel_id=1, source_target_pairs={{0,16},{16,32},{32,48},{48,64},{64,80},{80,96},{96,112},{1,17},{17... | collective-permute-start | bytes 1179656 | tf_op jit(solution)/shard_map/ppermute | solution.py:25
  916.9 38.8 %collective-permute-start.27 = (bf16[1,1,768,256]{2,3,1,0:T(8,128)(2,1)S(1)}, bf16[1,1,768,256]{2,3,1,0:T(8,128)(2,1)S(1)}, u32[]{:S(2)}, u32[]{:S(2)}) collective-permute-start(bf16[1,1,768,256]{2,3,1,0:T(8,128)(2,1)S(1)} %convert_bitcast_fusion), channel_id=1, source_target_pairs={{16,0},{32,16},{48,32},{64,48},{80,64},{96,80},{112,96},{17,1},{33... | collective-permute-start | bytes 1179656 | tf_op jit(solution)/shard_map/ppermute | solution.py:28
  919.3 49.5 %collective-permute-start.38 = (bf16[7,256,256]{1,2,0:T(8,128)(2,1)}, bf16[7,256,256]{1,2,0:T(8,128)(2,1)}, u32[]{:S(2)}, u32[]{:S(2)}) collective-permute-start(bf16[7,256,256]{1,2,0:T(8,128)(2,1)} %bitcast_dynamic-update-slice_fusion.19), channel_id=1, source_target_pairs={{0,16},{16,32},{32,48},{48,64},{64,80},{80,96},{96,112},{1,17},{17... | collective-permute-start | bytes 2752520 | tf_op jit(solution)/shard_map/ppermute | solution.py:17
  953.7 23.7 %collective-permute-start.39 = (bf16[7,256,256]{1,2,0:T(8,128)(2,1)}, bf16[7,256,256]{1,2,0:T(8,128)(2,1)S(1)}, u32[]{:S(2)}, u32[]{:S(2)}) collective-permute-start(bf16[7,256,256]{1,2,0:T(8,128)(2,1)} %bitcast_dynamic-update-slice_fusion.19), channel_id=1, source_target_pairs={{16,0},{32,16},{48,32},{64,48},{80,64},{96,80},{112,96},{17,1},{33... | collective-permute-start | bytes 2752520 | tf_op jit(solution)/shard_map/ppermute | solution.py:17
  955.7 25.7 %collective-permute-start.40 = (bf16[7,256,256]{1,2,0:T(8,128)(2,1)}, bf16[7,256,256]{1,2,0:T(8,128)(2,1)S(1)}, u32[]{:S(2)}, u32[]{:S(2)}) collective-permute-start(bf16[7,256,256]{1,2,0:T(8,128)(2,1)} %bitcast_dynamic-update-slice_fusion.19), channel_id=1, source_target_pairs={{32,0},{48,16},{64,32},{80,48},{96,64},{112,80},{33,1},{49,17},{65... | collective-permute-start | bytes 2752520 | tf_op jit(solution)/shard_map/ppermute | solution.py:17
  958.1 24.2 %collective-permute-start.41 = (bf16[7,256,256]{1,2,0:T(8,128)(2,1)}, bf16[7,256,256]{1,2,0:T(8,128)(2,1)S(1)}, u32[]{:S(2)}, u32[]{:S(2)}) collective-permute-start(bf16[7,256,256]{1,2,0:T(8,128)(2,1)} %bitcast_dynamic-update-slice_fusion.19), channel_id=1, source_target_pairs={{48,0},{64,16},{80,32},{96,48},{112,64},{49,1},{65,17},{81,33},{97... | collective-permute-start | bytes 2752520 | tf_op jit(solution)/shard_map/ppermute | solution.py:17
  961.6 37.9 %collective-permute-start.28 = (bf16[3,1,768,256]{2,3,1,0:T(8,128)(2,1)}, bf16[3,1,768,256]{2,3,1,0:T(8,128)(2,1)}, u32[]{:S(2)}, u32[]{:S(2)}) collective-permute-start(bf16[3,1,768,256]{2,3,1,0:T(8,128)(2,1)} %pad_maximum_fusion.3), channel_id=1, source_target_pairs={{0,1},{1,2},{2,3},{3,4},{4,5},{5,6},{6,7},{7,8},{8,9},{9,10},{10,1... | collective-permute-start | bytes 3538952 | tf_op jit(solution)/shard_map/ppermute | solution.py:25
  968.8 30.7 %collective-permute-start.29 = (bf16[3,1,768,256]{2,3,1,0:T(8,128)(2,1)}, bf16[3,1,768,256]{2,3,1,0:T(8,128)(2,1)}, u32[]{:S(2)}, u32[]{:S(2)}) collective-permute-start(bf16[3,1,768,256]{2,3,1,0:T(8,128)(2,1)} %pad_maximum_fusion.3), channel_id=1, source_target_pairs={{1,0},{2,1},{3,2},{4,3},{5,4},{6,5},{7,6},{8,7},{9,8},{10,9},{11,1... | collective-permute-start | bytes 3538952 | tf_op jit(solution)/shard_map/ppermute | solution.py:28
  1014.8 337.4 %all-reduce.17.cloned.1.call-start = ((), (), s32[]{:S(2)}) async-start(), calls=%async_computation.4 | async-start | bytes 524288 | tf_op jit(solution)/shard_map/psum | solution.py:161
  (68 other events, 1610.1 us)
Sparse Core Ops, SparseCore 0:
  12.1 144.7 all-reduce.8
  421.4 192.5 all-reduce.10
  618.8 138.9 all-reduce.12
  1015.0 191.7 all-reduce.14
  1212.1 140.1 all-reduce.16
where the time goes:
time: 1570 us; the launch traced here: 1560 us
  waiting for transfers between devices  888 us (57%)
  other arithmetic  300 us (19%)
  local copies, waits for them, and re-layouts  126 us (8%)
  starting transfers between devices  118 us (8%)
  matrix products  86.2 us (5%)
  between operations  37.7 us (2%)
    psum x2, waiting for transfers between devices, on_device(): projected = lax.psum(local_gram(stacked, image), ('wide', 'col'))  382 us
    psum x2, waiting for transfers between devices, on_device(): gram_sum = lax.psum(local_gram(image, image), ('wide', 'col'))  270 us
    psum x1, waiting for transfers between devices, on_device(): first_sum = lax.psum(local_gram(rhs, rhs), ('wide', 'col'))  147 us
    ppermute x34, starting transfers between devices, passed_along(): return lax.ppermute(block, axis, route)  95.2 us
    another operation x15, other arithmetic, on_device(): small_factor = jnp.linalg.cholesky(normal_matrix)  79.5 us
    another operation x14, other arithmetic, on_device(): factor = jnp.linalg.cholesky(gram_sum)  76.6 us
    ppermute x4, waiting for transfers between devices, with_halo(): lax.ppermute(lax.slice_in_dim(block, block.shape[dim] - width, None, axis...  50.4 us
    another operation x4, other arithmetic, lower_solve(): lax.linalg.triangular_solve(factor, matrix, left_side=False, lower=True,...  42.9 us
  transfers between devices with their start and end apart: 47, of which 21 were waited for; matrix products, arithmetic and copies ran while one was open for 6% of the time, Pallas kernels for 0%

commit v1 on v0

v1 whole, which is shorter than its diff:
```python
import functools

import jax
import jax.numpy as jnp
from jax import lax
from jax.experimental import pallas as pl
from jax.experimental.pallas import tpu as pltpu
from jax.sharding import PartitionSpec as P

REACH = 3
SPAN = 2 * REACH + 1
MESH = pl.DeviceIdType.MESH
HIGHEST = lax.Precision.HIGHEST
F32 = jnp.float32
BF16 = jnp.bfloat16
VMEM_BYTES = 60 * 1024 * 1024


def dot(left, right):
    return jnp.dot(left, right, preferred_element_type=F32)


def dot_full(left, right):
    return jnp.dot(left, right, precision=HIGHEST, preferred_element_type=F32)


def dot_full_t(left, right):
    return lax.dot_general(
        left, right, (((1,), (1,)), ((), ())), precision=HIGHEST, preferred_element_type=F32
    )


def t_dot_full(left, right):
    return lax.dot_general(
        left, right, (((0,), (0,)), ((), ())), precision=HIGHEST, preferred_element_type=F32
    )


def picks(start, count, total):
    row = lax.broadcasted_iota(jnp.int32, (count, total), 0)
    lane = lax.broadcasted_iota(jnp.int32, (count, total), 1)
    return jnp.where(lane - row == start, 1.0, 0.0).astype(BF16)


def places(start, count, total):
    row = lax.broadcasted_iota(jnp.int32, (total, count), 0)
    lane = lax.broadcasted_iota(jnp.int32, (total, count), 1)
    return jnp.where(row - lane == start, 1.0, 0.0).astype(BF16)


def three_parts(value):
    high = value.astype(BF16)
    rest = value - high.astype(F32)
    mid = rest.astype(BF16)
    return high, mid, (rest - mid.astype(F32)).astype(BF16)


def remote(src, dst, send_sem, recv_sem, w, c):
    return pltpu.make_async_remote_copy(
        src_ref=src,
        dst_ref=dst,
        send_sem=send_sem,
        recv_sem=recv_sem,
        device_id=(w, c),
        device_id_type=MESH,
    )


def greet(w, c, wide, col):
    barrier = pltpu.get_barrier_semaphore()

    def along_col(k, carry):
        pl.semaphore_signal(
            barrier, inc=1, device_id=(w, lax.rem(c + k, col)), device_id_type=MESH
        )
        return carry

    def along_wide(k, carry):
        pl.semaphore_signal(
            barrier, inc=1, device_id=(lax.rem(w + k, wide), c), device_id_type=MESH
        )
        return carry

    lax.fori_loop(1, col, along_col, 0)
    lax.fori_loop(1, wide, along_wide, 0)


def meet(wide, col):
    pl.semaphore_wait(pltpu.get_barrier_semaphore(), wide + col - 2)


def all_reduce(w, c, wide, col, g, half, land, ysl, out, send, recv):
    rows = g.shape[0]
    high = rows // 2
    part = high // col
    core = lax.rem(w, 2)
    y = w // 2
    ys = wide // 2
    partner = w + 1 - 2 * core
    mine = pl.multiple_of(core * high, high)
    other = pl.multiple_of((1 - core) * high, high)
    own = pl.multiple_of(mine + c * part, part)

    swap = remote(g.at[pl.ds(other, high)], half, send.at[0], recv.at[0], partner, c)
    swap.start()
    swap.wait()
    g[pl.ds(mine, high), :] += half[...]

    def scatter(k, carry):
        d = lax.rem(c + k, col)
        remote(
            g.at[pl.ds(pl.multiple_of(mine + d * part, part), part)],
            land.at[pl.ds(pl.multiple_of((col - 1 - k) * part, part), part)],
            send.at[1],
            recv.at[1],
            w,
            d,
        ).start()
        return carry

    lax.fori_loop(1, col, scatter, 0)
    many = (col - 1) * part
    remote(g.at[pl.ds(0, many)], land, send.at[1], recv.at[1], w, c).wait()
    total = g[pl.ds(own, part), :]
    for k in range(col - 1):
        total += land[k * part : (k + 1) * part, :]
    ysl[y] = total

    def spread(k, carry):
        other_y = lax.rem(y + k, ys)
        remote(ysl.at[y], ysl.at[y], send.at[2], recv.at[2], 2 * other_y + core, c).start()
        return carry

    lax.fori_loop(1, ys, spread, 0)
    few = pl.ds(0, ys - 1)
    remote(ysl.at[few], ysl.at[few], send.at[2], recv.at[2], w, c).wait()
    total = ysl[0]
    for k in range(1, ys):
        total += ysl[k]
    out[pl.ds(own, part), :] = total

    def gather(k, carry):
        d = lax.rem(c + k, col)
        spot = pl.ds(own, part)
        remote(out.at[spot], out.at[spot], send.at[3], recv.at[3], w, d).start()
        return carry

    lax.fori_loop(1, col, gather, 0)
    spot = pl.ds(0, many)
    remote(out.at[spot], out.at[spot], send.at[3], recv.at[3], w, c).wait()
    spot = pl.ds(mine, high)
    swap = remote(out.at[spot], out.at[spot], send.at[4], recv.at[4], partner, c)
    swap.start()
    swap.wait()


def reduce_scratch(rows, width, wide, col):
    high = rows // 2
    part = high // col
    return [
        pltpu.VMEM((rows, width), F32),
        pltpu.VMEM((high, width), F32),
        pltpu.VMEM(((col - 1) * part, width), F32),
        pltpu.VMEM((wide // 2, part, width), F32),
        pltpu.SemaphoreType.DMA((5,)),
        pltpu.SemaphoreType.DMA((5,)),
    ]


def local_grams(lefts, right, g, step):
    width = right.shape[1]
    rows = right.shape[0]
    for i, left in enumerate(lefts):
        spot = slice(i * width, (i + 1) * width)
        g[spot, :] = t_dot_full(left[0:step, :], right[0:step, :])

        def add(k, carry, left=left, spot=spot):
            piece = pl.ds(pl.multiple_of(k * step, step), step)
            g[spot, :] += t_dot_full(left[piece, :], right[piece, :])
            return carry

        lax.fori_loop(1, rows // step, add, 0)


def first_gram_kernel(wide, col, step, rhs, out, g, half, land, ysl, send, recv):
    w, c = lax.axis_index("wide"), lax.axis_index("col")
    greet(w, c, wide, col)
    local_grams([rhs], rhs, g, step)
    meet(wide, col)
    all_reduce(w, c, wide, col, g, half, land, ysl, out, send, recv)


def step_kernel(wide, col, step, first, *refs):
    if first:
        (starts, near_ids, far_ids, x, mt, basis_h, self_h, near_h, coup_h, sch_h, *rest) = refs
        (v, z, wv, gram, *rest) = rest
    else:
        (starts, near_ids, far_ids, x, mt, vprev, u, basis_h, self_h, near_h, coup_h, sch_h, *rest) = refs
        (z, gram, v, wv, *rest) = rest
    (basis, selfb, near, coup, sch, stage, dom, pad_next, pad_prev, edge, nb, win, far, *rest) = rest
    (load, hs, hr, ns, nr, ws, wr, rs, rr, ps, pr, *reduce) = rest
    g, half, land, ysl, send, recv = reduce
    w, c = lax.axis_index("wide"), lax.axis_index("col")
    core = lax.rem(w, 2)
    partner = w + 1 - 2 * core
    rows, width = x.shape
    margin = edge.shape[1]
    has_prev, has_next = c > 0, c < col - 1

    loads = [
        pltpu.make_async_copy(sch_h.at[0], sch, load.at[0]),
        pltpu.make_async_copy(basis_h, basis, load.at[1]),
        pltpu.make_async_copy(self_h, selfb, load.at[2]),
        pltpu.make_async_copy(near_h.at[0], near, load.at[3]),
        pltpu.make_async_copy(coup_h.at[0], coup, load.at[4]),
    ]
    for copy in loads:
        copy.start()

    @pl.when(jnp.logical_not(has_prev))
    def _():
        dom[0:margin, :] = jnp.zeros((margin, width), BF16)
        pad_prev[...] = jnp.zeros((margin, width), F32)

    @pl.when(jnp.logical_not(has_next))
    def _():
        dom[margin + rows :, :] = jnp.zeros((margin, width), BF16)
        pad_next[...] = jnp.zeros((margin, width), F32)

    greet(w, c, wide, col)

    def make_v(k, carry):
        piece = pl.ds(pl.multiple_of(k * step, step), step)
        value = dot_full(x[piece, :], mt[...])
        if not first:
            value += dot_full(vprev[piece, :], u[...])
        v[piece, :] = value
        dom[pl.ds(pl.multiple_of(margin + k * step, step), step), :] = value.astype(BF16)
        return carry

    lax.fori_loop(0, rows // step, make_v, 0)
    start_prev, start_next = starts[0, 0], starts[0, 1]
    stage[0] = dot(picks(start_next, margin, rows), dom[margin : margin + rows, :]).astype(BF16)
    stage[1] = dot(picks(start_prev, margin, rows), dom[margin : margin + rows, :]).astype(BF16)
    meet(wide, col)

    to_next = remote(stage.at[0], dom.at[pl.ds(0, margin)], hs.at[0], hr.at[0], w, c + 1)
    to_prev = remote(
        stage.at[1], dom.at[pl.ds(margin + rows, margin)], hs.at[1], hr.at[1], w, c - 1
    )
    out_prev = remote(
        edge.at[0], pad_next, hs.at[2], hr.at[2], w, c - 1
    )
    out_next = remote(
        edge.at[1], pad_prev, hs.at[3], hr.at[3], w, c + 1
    )
    pl.when(has_next)(to_next.start)
    pl.when(has_prev)(to_prev.start)

    nb[9] = jnp.zeros((rows, width), BF16)
    win[SPAN * SPAN] = jnp.zeros(win.shape[1:], BF16)

    loads[0].wait()
    pl.when(has_prev)(to_next.wait_recv)
    pl.when(has_next)(to_prev.wait_recv)
    edge[0] = dot(sch[0:margin, :], dom[...])
    pl.when(has_prev)(out_prev.start)
    edge[1] = dot(sch[margin + rows :, :], dom[...])
    pl.when(has_next)(out_next.start)

    def solve(k, carry):
        piece = pl.ds(pl.multiple_of(k * step, step), step)
        z[piece, :] = dot(sch[pl.ds(pl.multiple_of(margin + k * step, step), step), :], dom[...])
        return carry

    lax.fori_loop(0, rows // step, solve, 0)
    pl.when(has_next)(out_prev.wait_recv)
    pl.when(has_prev)(out_next.wait_recv)
    for start, pad in ((start_next, pad_next), (start_prev, pad_prev)):
        spread = places(start, margin, rows)
        for part in three_parts(pad[...]):
            z[...] += dot(spread, part)
    nb[4] = z[...].astype(BF16)
    loads[1].wait()

    def near_to(dw, dc, source):
        return remote(
            nb.at[source], nb.at[(1 - dw) * 3 + dc + 1], ns.at[(1 - dw) * 3 + dc + 1],
            nr.at[(1 - dw) * 3 + dc + 1], w + dw, c,
        )

    def near_col(dc):
        return remote(nb.at[4], nb.at[4 - dc], ns.at[4 - dc], nr.at[4 - dc], w, c + dc)

    beside = {-1: has_prev, 1: has_next}
    within = {d: (w + d >= 0) & (w + d < wide) for d in range(-REACH, REACH + 1) if d}
    for d in (-1, 1):
        pl.when(beside[d])(near_col(d).start)
    for d in (-1, 1):
        pl.when(within[d])(near_to(d, 0, 4).start)

    centre = REACH * SPAN + REACH
    win[centre] = lax.dot_general(
        basis[...], nb[4], (((0,), (0,)), ((), ())), preferred_element_type=F32
    ).astype(BF16)

    def far_wide(d):
        return remote(
            win.at[centre], win.at[centre - d], ws.at[REACH - d], wr.at[REACH - d], w + d, c
        )

    for d in (1, -1, 2, -2, 3, -3):
        pl.when(within[d])(far_wide(d).start)

    loads[2].wait()

    def own_part(k, carry):
        piece = pl.ds(pl.multiple_of(k * step, step), step)
        wv[piece, :] = dot(selfb[piece, :], nb[4])
        return carry

    lax.fori_loop(0, rows // step, own_part, 0)

    for d in within:
        pl.when(within[-d])(far_wide(d).wait_recv)

    def strip_to(direction, k):
        held = REACH - direction * (k - 1)
        lands = held - direction
        rows_of = lambda i: pl.ds(i * SPAN + REACH * core, REACH + 1)
        sem = lands
        return remote(
            win.at[rows_of(held)], win.at[rows_of(lands)], rs.at[sem], rr.at[sem], w, c + direction
        )

    def share(i):
        return remote(
            win.at[pl.ds(i * SPAN + 1 + 2 * core, REACH)],
            win.at[pl.ds(i * SPAN + (REACH + 1) * core, REACH)],
            ps.at[i], pr.at[i], partner, c,
        )

    def arrives(direction, k):
        return c - k >= 0 if direction > 0 else c + k < col

    def sends(direction, k):
        held = c - (k - 1) >= 0 if direction > 0 else c + (k - 1) < col
        return held & beside[direction]

    for d in (1, -1):
        pl.when(sends(d, 1))(strip_to(d, 1).start)

    for d in (-1, 1):
        pl.when(beside[d])(near_col(-d).wait_recv)
        for e in (-1, 1):
            pl.when(beside[d] & within[e])(near_to(e, d, 4 + d).start)

    for k in range(1, REACH + 1):
        for d in (1, -1):
            pl.when(arrives(d, k))(strip_to(d, k).wait_recv)
            if k < REACH:
                pl.when(sends(d, k + 1))(strip_to(d, k + 1).start)
            pl.when(arrives(d, k))(share(REACH - d * k).start)
        if k == 1:
            for e in (-1, 1):
                for d in (-1, 0, 1):
                    ok = within[-e] if d == 0 else within[-e] & beside[d]
                    pl.when(ok)(near_to(e, d, 4 + d).wait_recv)
            loads[3].wait()

            def near_slot(s, carry):
                cluster = near_ids[0, s]
                place = (lax.div(cluster, col) - w + 1) * 3 + (lax.rem(cluster, col) - c + 1)
                place = jnp.where(cluster >= 0, jnp.minimum(jnp.maximum(place, 0), 8), 9)

                def near_rows(r, inner):
                    piece = pl.ds(pl.multiple_of(r * step, step), step)
                    wv[piece, :] += dot(near[s, piece, :], nb[place])
                    return inner

                return lax.fori_loop(0, rows // step, near_rows, carry)

            lax.fori_loop(0, near_ids.shape[1], near_slot, 0)
    for k in range(1, REACH + 1):
        for d in (1, -1):
            pl.when(arrives(d, k))(share(REACH - d * k).wait_recv)
    loads[4].wait()
    far[...] = jnp.zeros_like(far)

    def far_slot(s, carry):
        cluster = far_ids[0, s]
        place = (lax.rem(cluster, col) - c + REACH) * SPAN + (lax.div(cluster, col) - w + REACH)
        place = jnp.where(cluster >= 0, jnp.minimum(jnp.maximum(place, 0), SPAN * SPAN - 1), SPAN * SPAN)
        far[...] += dot(coup[s], win[place])
        return carry

    lax.fori_loop(0, far_ids.shape[1], far_slot, 0)
    far_b = far[...].astype(BF16)

    def basis_part(k, carry):
        piece = pl.ds(pl.multiple_of(k * step, step), step)
        wv[piece, :] += dot(basis[piece, :], far_b)
        return carry

    lax.fori_loop(0, rows // step, basis_part, 0)
    local_grams([v, wv] if first else [vprev, x, wv], wv, g, step)

    pl.when(has_next)(to_next.wait_send)
    pl.when(has_prev)(to_prev.wait_send)
    pl.when(has_prev)(out_prev.wait_send)
    pl.when(has_next)(out_next.wait_send)
    for d in (-1, 1):
        pl.when(beside[d])(near_col(d).wait_send)
        pl.when(within[d])(near_to(d, 0, 4).wait_send)
        for e in (-1, 1):
            pl.when(beside[d] & within[e])(near_to(e, d, 4 + d).wait_send)
    for d in within:
        pl.when(within[d])(far_wide(d).wait_send)
    for k in range(1, REACH + 1):
        for d in (1, -1):
            pl.when(sends(d, k))(strip_to(d, k).wait_send)
            pl.when(arrives(d, k))(share(REACH - d * k).wait_send)

    all_reduce(w, c, wide, col, g, half, land, ysl, gram, send, recv)


def inverse_factors(matrices, scratch):
    n = matrices[0].shape[0]
    row = lax.broadcasted_iota(jnp.int32, (n, n), 0)
    lane = lax.broadcasted_iota(jnp.int32, (n, n), 1)
    eye = (row == lane).astype(F32)

    def lower(e):
        return jnp.where(row > lane, e, 0.5 * e * eye)

    scaled, scales = [], []
    for i, a in enumerate(matrices):
        only = a * eye
        by_row = lax.rsqrt(jnp.sum(only, axis=1, keepdims=True))
        by_lane = lax.rsqrt(jnp.sum(only, axis=0, keepdims=True))
        a = a * by_row * by_lane
        scratch[i] = eye - lower(a - eye)
        scaled.append(a)
        scales.append(by_lane)
    limit = 1e-5

    def go_on(state):
        step, error = state
        return (step < 8) & jnp.logical_not(error < limit)

    def refine(state):
        step, _ = state
        error = jnp.float32(0.0)
        for i, a in enumerate(scaled):
            m = scratch[i]
            e = dot_full_t(dot_full(m, a), m) - eye
            scratch[i] = m - dot_full(lower(e), m)
            error = error + jnp.sum(e * e)
        return step + 1, error

    _, error = lax.while_loop(go_on, refine, (jnp.int32(0), jnp.float32(1.0)))

    @pl.when(jnp.logical_not(error < limit))
    def _():
        for i, a in enumerate(scaled):

            def eliminate(j, state):
                s, m = state
                at_lane = jnp.sum(jnp.where(lane == j, s, 0.0), axis=1, keepdims=True)
                at_row = jnp.sum(jnp.where(row == j, s, 0.0), axis=0, keepdims=True)
                m_row = jnp.sum(jnp.where(row == j, m, 0.0), axis=0, keepdims=True)
                pivot = jnp.sum(jnp.where(row == j, at_lane, 0.0), axis=0, keepdims=True)
                pivot = pivot[:, 0:1]
                times = jnp.where(row[:, 0:1] > j, at_lane / pivot, 0.0)
                s = s - times * at_row
                m = m - times * m_row
                m = jnp.where(row == j, m_row * lax.rsqrt(pivot), m)
                return s, m

            _, m = lax.fori_loop(0, n, eliminate, (a, eye))
            scratch[i] = m

    for i, by_lane in enumerate(scales):
        scratch[i] = scratch[i] * by_lane


def first_factor_kernel(g0, m, mt):
    inverse_factors([g0[...]], m)
    mt[...] = m[0].T


def second_factor_kernel(gram, m, mt, u):
    k = gram.shape[1]
    h = gram[0:k, :]
    n = gram[k:, :]
    inverse_factors([n - t_dot_full(h, h), n], m)
    mt[...] = m[0].T
    u[...] = -dot_full(h, mt[...])


def last_kernel(step, g0, m0, gram1, mn, gram2, z1, z2, out, m):
    k = g0.shape[1]
    beta = dot_full(m0[0], g0[...])
    h1, h2 = gram1[0:k, :], gram2[0:k, :]
    n12, n22 = gram2[k : 2 * k, :], gram2[2 * k :, :]
    first = mn[1]
    b1 = dot_full(first, t_dot_full(h1, beta))
    t = dot_full(first, n12)
    inverse_factors([n22 - t_dot_full(t, t)], m)
    b2 = t_dot_full(h2, beta) - t_dot_full(t, b1)
    y2 = t_dot_full(m[0], dot_full(m[0], b2))
    y1 = t_dot_full(first, b1 - dot_full(t, y2))

    def combine(i, carry):
        piece = pl.ds(pl.multiple_of(i * step, step), step)
        out[piece, :] = dot_full(z1[piece, :], y1) + dot_full(z2[piece, :], y2)
        return carry

    lax.fori_loop(0, out.shape[0] // step, combine, 0)


def on_device(
    wide, col, rhs, basis, self_block, near_block, near_ids, couplings, far_ids, starts, schwarz_inverse
):
    rows, width = rhs.shape
    rank = basis.shape[1]
    order = schwarz_inverse.shape[1]
    margin = (order - rows) // 2
    step = rows // 3
    slots, links = near_ids.shape[1], far_ids.shape[1]
    vmem = pl.BlockSpec(memory_space=pltpu.VMEM)
    smem = pl.BlockSpec(memory_space=pltpu.SMEM)
    anywhere = pl.BlockSpec(memory_space=pl.ANY)

    def block(n):
        return jax.ShapeDtypeStruct((n, width), F32)

    square = jax.ShapeDtypeStruct((1, width, width), F32)
    local = pltpu.CompilerParams(vmem_limit_bytes=VMEM_BYTES)

    def talks(number):
        return pltpu.CompilerParams(
            collective_id=number, has_side_effects=True, vmem_limit_bytes=VMEM_BYTES
        )

    gram0 = pl.pallas_call(
        functools.partial(first_gram_kernel, wide, col, step),
        out_shape=block(width),
        in_specs=[vmem],
        out_specs=vmem,
        scratch_shapes=reduce_scratch(width, width, wide, col),
        compiler_params=talks(0),
        name="first_gram",
    )(rhs)
    m0, mt0 = pl.pallas_call(
        first_factor_kernel,
        out_shape=(square, block(width)),
        in_specs=[vmem],
        out_specs=(vmem, vmem),
        compiler_params=local,
        name="first_factor",
    )(gram0)

    def take_step(first, *blocks):
        grams = 2 if first else 3
        outs = [block(rows)] * 3 if first else [block(rows)]
        held = [] if first else [pltpu.VMEM((rows, width), F32)] * 2
        dma = pltpu.SemaphoreType.DMA
        return pl.pallas_call(
            functools.partial(step_kernel, wide, col, step, first),
            out_shape=(*outs, block(grams * width)),
            in_specs=[smem] * 3 + [vmem] * len(blocks) + [anywhere] * 5,
            out_specs=(vmem,) * (len(outs) + 1),
            scratch_shapes=held
            + [
                pltpu.VMEM((rows, rank), BF16),
                pltpu.VMEM((rows, rows), BF16),
                pltpu.VMEM((slots, rows, rows), BF16),
                pltpu.VMEM((links, rank, rank), BF16),
                pltpu.VMEM((order, order), BF16),
                pltpu.VMEM((2, margin, width), BF16),
                pltpu.VMEM((order, width), BF16),
                pltpu.VMEM((margin, width), F32),
                pltpu.VMEM((margin, width), F32),
                pltpu.VMEM((2, margin, width), F32),
                pltpu.VMEM((10, rows, width), BF16),
                pltpu.VMEM((SPAN * SPAN + 1, rank, width), BF16),
                pltpu.VMEM((rank, width), F32),
                dma((5,)),
                dma((4,)),
                dma((4,)),
                dma((9,)),
                dma((9,)),
                dma((SPAN,)),
                dma((SPAN,)),
                dma((SPAN,)),
                dma((SPAN,)),
                dma((SPAN,)),
                dma((SPAN,)),
            ]
            + reduce_scratch(grams * width, width, wide, col),
            compiler_params=talks(1 if first else 2),
            name="first_step" if first else "second_step",
        )(starts, near_ids, far_ids, *blocks, basis, self_block, near_block, couplings, schwarz_inverse)

    v1, z1, w1, gram1 = take_step(True, rhs, mt0)
    m1, mt1, u = pl.pallas_call(
        second_factor_kernel,
        out_shape=(jax.ShapeDtypeStruct((2, width, width), F32), block(width), block(width)),
        in_specs=[vmem],
        out_specs=(vmem,) * 3,
        compiler_params=local,
        name="second_factor",
    )(gram1)
    z2, gram2 = take_step(False, w1, mt1, v1, u)
    return pl.pallas_call(
        functools.partial(last_kernel, step),
        out_shape=block(rows),
        in_specs=[vmem] * 7,
        out_specs=vmem,
        scratch_shapes=[pltpu.VMEM((1, width, width), F32)],
        compiler_params=local,
        name="last",
    )(gram0, m0, gram1, m1, gram2, z1, z2)


def solution(mesh):
    in_specs = (
        P(("wide", "col"), None),
        P(("wide", "col"), None),
        P(("wide", "col"), None),
        P(("wide", "col"), None, None, None),
        P(("wide", "col"), None),
        P(("wide", "col"), None, None, None),
        P(("wide", "col"), None),
        P(("wide", "col"), None),
        P(("wide", "col"), None, None),
    )
    out_specs = P(("wide", "col"), None)
    return jax.shard_map(
        functools.partial(on_device, mesh.shape["wide"], mesh.shape["col"]),
        mesh=mesh,
        in_specs=in_specs,
        out_specs=out_specs,
        check_vma=False,
    )
```

time: 1570 us -> 345 us (0.22)
  waiting for transfers between devices: 888 us -> 0 us
  Pallas kernels: 0 us -> 344 us
  other arithmetic: 300 us -> 0 us
  local copies, waits for them, and re-layouts: 126 us -> 0 us
  starting transfers between devices: 118 us -> 0 us
  matrix products: 86.2 us -> 0 us
  between operations: 37.7 us -> 0.03 us
    psum x5 -> x0, waiting for transfers between devices: 799 us -> none  [the longest x2 382 us: on_device(): projected = lax.psum(local_gram(stacked, image), ('wide', 'col'))]
    pallas_call x0 -> x6, Pallas kernels: none -> 344 us  [the longest x2 210 us: take_step(): pl.pallas_call(functools.partial(step_kernel, wide, col, step, first), ou...]
    another operation x47 -> x0, other arithmetic: 282 us -> none  [the longest x15 79.5 us: on_device(): small_factor = jnp.linalg.cholesky(normal_matrix)]
    ppermute x42 -> x0, starting transfers between devices: 117 us -> none  [the longest x34 95.2 us: passed_along(): return lax.ppermute(block, axis, route)]
    ppermute x42 -> x0, waiting for transfers between devices: 88.8 us -> none  [the longest x4 50.4 us: with_halo(): lax.ppermute(lax.slice_in_dim(block, block.shape[dim] - width, None, axis...]
    dot_general x36 -> x0, matrix products: 56.3 us -> none  [the longest x16 19.5 us: operate(): jnp.dot(near_block[0, slot_index], other, preferred_element_type=jnp.floa...]
    unnamed x114 -> x0, local copies, waits for them, and re-layouts: 37 us -> none
    another operation x47 -> x0, local copies, waits for them, and re-layouts: 35.1 us -> none  [the longest x15 15.4 us: lower_solve(): lax.linalg.triangular_solve(factor, matrix, left_side=False, lower=True,...]
  transfers between devices with their start and end apart: 47 -> 0, of which waited for: 21 -> 0; matrix products, arithmetic and copies ran while one was open for 6% -> 0% of each run, Pallas kernels for 0% -> 0%
where the time goes in v1:
time: 345 us; the launch traced here: 344 us
  Pallas kernels  344 us (100%)
    pallas_call x2, Pallas kernels, take_step(): pl.pallas_call(functools.partial(step_kernel, wide, col, step, first), ou...  210 us
    pallas_call x1, Pallas kernels, on_device(): pl.pallas_call(first_factor_kernel, out_shape=(square, block(width)), in_...  87.8 us
    pallas_call x1, Pallas kernels, on_device(): pl.pallas_call(functools.partial(first_gram_kernel, wide, col, step), out...  27 us
    pallas_call x1, Pallas kernels, on_device(): pl.pallas_call(functools.partial(last_kernel, step), out_shape=block(rows...  12.2 us
    pallas_call x1, Pallas kernels, on_device(): pl.pallas_call(second_factor_kernel, out_shape=(jax.ShapeDtypeStruct((2,...  7.7 us

profile of v1, /device:TPU:1, one launch (start us, length us, event | category | flops | bytes accessed | tf_op | source)
XLA Modules:
  0.0 344.3 jit_solution(6567625123813831117)
XLA Ops:
  0.0 27.0 %first_gram.1.g0 = f32[256,256]{1,0:T(8,128)} custom-call(f32[768,256]{1,0:T(8,128)} %refs_3_.1), custom_call_target="tpu_custom_call" | custom-call | tf_op jit(solution)/shard_map/first_gram/pallas_call | solution.py:546
  27.0 87.8 %first_factor.1 = (f32[1,256,256]{2,1,0:T(8,128)}, f32[256,256]{1,0:T(8,128)}) custom-call(f32[256,256]{1,0:T(8,128)} %first_gram.1.g0), custom_call_target="tpu_custom_call" | custom-call | tf_op jit(solution)/shard_map/first_factor/pallas_call | solution.py:555
  114.7 102.3 %first_step.1 = (f32[768,256]{1,0:T(8,128)}, f32[768,256]{1,0:T(8,128)}, f32[768,256]{1,0:T(8,128)}, f32[512,256]{1,0:T(8,128)}) custom-call(s32[1,2]{1,0:T(1,128)} %refs_0_.3, s32[1,8]{1,0:T(1,128)} %refs_1_.3, s32[1,40]{1,0:T(1,128)} %refs_2_.3, f32[768,256]{1,0:T(8,128)} %refs_3_.1, f32[256,256]{1,0:T(8,128)} %get-tuple-element.17.refs_4_, ...), custom_call_target="tpu_custom_call" | custom-call | tf_op jit(solution)/shard_map/first_step/pallas_call | solution.py:569
  217.1 7.7 %second_factor.1 = (f32[2,256,256]{2,1,0:T(8,128)}, f32[256,256]{1,0:T(8,128)}, f32[256,256]{1,0:T(8,128)}) custom-call(f32[512,256]{1,0:T(8,128)} %get-tuple-element.18.gram.gram1), custom_call_target="tpu_custom_call" | custom-call | tf_op jit(solution)/shard_map/second_factor/pallas_call | solution.py:607
  224.8 107.3 %second_step.1 = (f32[768,256]{1,0:T(8,128)}, f32[768,256]{1,0:T(8,128)}) custom-call(s32[1,2]{1,0:T(1,128)} %refs_0_.3, s32[1,8]{1,0:T(1,128)} %refs_1_.3, s32[1,40]{1,0:T(1,128)} %refs_2_.3, f32[768,256]{1,0:T(8,128)} %get-tuple-element.20.refs_3_, f32[256,256]{1,0:T(8,128)} %get-tuple-element.21.refs_4_, f32[768,256]{1,0:T(8,128)} %get-tuple-element.22.refs_5_, ...), custom_call_target="tpu_custom_call" | custom-call | tf_op jit(solution)/shard_map/second_step/pallas_call | solution.py:569
  332.1 12.2 %last.1 = f32[768,256]{1,0:T(8,128)} custom-call(f32[256,256]{1,0:T(8,128)} %first_gram.1.g0, f32[1,256,256]{2,1,0:T(8,128)} %get-tuple-element.16.m0, f32[512,256]{1,0:T(8,128)} %get-tuple-element.18.gram.gram1, f32[2,256,256]{2,1,0:T(8,128)} %get-tuple-element.19.mn, f32[768,256]{1,0:T(8,128)} %get-tuple-element.24.gram2, ...), custom_call_target="tpu_custom_call" | custom-call | tf_op jit(solution)/shard_map/last/pallas_call | solution.py:616

commit v2 on v1

--- a/solution.py
+++ b/solution.py
@@ -34,6 +34,21 @@
     return lax.dot_general(
         left, right, (((0,), (0,)), ((), ())), precision=HIGHEST, preferred_element_type=F32
     )
+
+
+def two_parts(value):
+    high = value.astype(BF16)
+    return high, (value - high.astype(F32)).astype(BF16)
+
+
+def dot_three(left, right, dims=((1,), (0,))):
+    lh, ll = two_parts(left)
+    rh, rl = two_parts(right)
+
+    def one(a, b):
+        return lax.dot_general(a, b, (dims, ((), ())), preferred_element_type=F32)
+
+    return (one(lh, rl) + one(ll, rh)) + one(lh, rh)
 
 
 def picks(start, count, total):
@@ -172,11 +187,11 @@
     rows = right.shape[0]
     for i, left in enumerate(lefts):
         spot = slice(i * width, (i + 1) * width)
-        g[spot, :] = t_dot_full(left[0:step, :], right[0:step, :])
+        g[spot, :] = dot_three(left[0:step, :], right[0:step, :], ((0,), (0,)))
 
         def add(k, carry, left=left, spot=spot):
             piece = pl.ds(pl.multiple_of(k * step, step), step)
-            g[spot, :] += t_dot_full(left[piece, :], right[piece, :])
+            g[spot, :] += dot_three(left[piece, :], right[piece, :], ((0,), (0,)))
             return carry
 
         lax.fori_loop(1, rows // step, add, 0)
@@ -192,10 +207,10 @@
 
 def step_kernel(wide, col, step, first, *refs):
     if first:
-        (starts, near_ids, far_ids, x, mt, basis_h, self_h, near_h, coup_h, sch_h, *rest) = refs
+        (starts, near_ids, order, x, mt, basis_h, self_h, near_h, coup_h, sch_h, *rest) = refs
         (v, z, wv, gram, *rest) = rest
     else:
-        (starts, near_ids, far_ids, x, mt, vprev, u, basis_h, self_h, near_h, coup_h, sch_h, *rest) = refs
+        (starts, near_ids, order, x, mt, vprev, u, basis_h, self_h, near_h, coup_h, sch_h, *rest) = refs
         (z, gram, v, wv, *rest) = rest
     (basis, selfb, near, coup, sch, stage, dom, pad_next, pad_prev, edge, nb, win, far, *rest) = rest
     (load, hs, hr, ns, nr, ws, wr, rs, rr, ps, pr, *reduce) = rest
@@ -212,7 +227,9 @@
         pltpu.make_async_copy(basis_h, basis, load.at[1]),
         pltpu.make_async_copy(self_h, selfb, load.at[2]),
         pltpu.make_async_copy(near_h.at[0], near, load.at[3]),
-        pltpu.make_async_copy(coup_h.at[0], coup, load.at[4]),
+        pltpu.make_async_copy(
+            coup_h.at[0], coup.at[pl.ds(0, coup_h.shape[1])], load.at[4]
+        ),
     ]
     for copy in loads:
         copy.start()
@@ -226,6 +243,16 @@
     def _():
         dom[margin + rows :, :] = jnp.zeros((margin, width), BF16)
         pad_next[...] = jnp.zeros((margin, width), F32)
+
+    for i in range(SPAN):
+        for a in range(SPAN):
+            dc, dw = i - REACH, a - REACH
+            off = (w + dw < 0) | (w + dw >= wide) | (c + dc < 0) | (c + dc >= col)
+            if (dw or dc) and max(abs(dw), abs(dc)) > 1:
+
+                @pl.when(off)
+                def _(cell=i * SPAN + a):
+                    win[cell] = jnp.zeros(win.shape[1:], BF16)
 
     greet(w, c, wide, col)
 
@@ -258,7 +285,6 @@
     pl.when(has_prev)(to_prev.start)
 
     nb[9] = jnp.zeros((rows, width), BF16)
-    win[SPAN * SPAN] = jnp.zeros(win.shape[1:], BF16)
 
     loads[0].wait()
     pl.when(has_prev)(to_next.wait_recv)
@@ -312,32 +338,22 @@
     for d in (1, -1, 2, -2, 3, -3):
         pl.when(within[d])(far_wide(d).start)
 
-    loads[2].wait()
-
-    def own_part(k, carry):
-        piece = pl.ds(pl.multiple_of(k * step, step), step)
-        wv[piece, :] = dot(selfb[piece, :], nb[4])
-        return carry
-
-    lax.fori_loop(0, rows // step, own_part, 0)
-
-    for d in within:
-        pl.when(within[-d])(far_wide(d).wait_recv)
-
-    def strip_to(direction, k):
+    def on_grid(a):
+        return (w + a - REACH >= 0) & (w + a - REACH < wide)
+
+    def hand_on(direction, k, j):
         held = REACH - direction * (k - 1)
         lands = held - direction
-        rows_of = lambda i: pl.ds(i * SPAN + REACH * core, REACH + 1)
-        sem = lands
+        a = REACH * core + j
         return remote(
-            win.at[rows_of(held)], win.at[rows_of(lands)], rs.at[sem], rr.at[sem], w, c + direction
+            win.at[held * SPAN + a], win.at[lands * SPAN + a],
+            rs.at[lands * (REACH + 1) + j], rr.at[lands * (REACH + 1) + j], w, c + direction,
         )
 
-    def share(i):
+    def share(i, j):
         return remote(
-            win.at[pl.ds(i * SPAN + 1 + 2 * core, REACH)],
-            win.at[pl.ds(i * SPAN + (REACH + 1) * core, REACH)],
-            ps.at[i], pr.at[i], partner, c,
+            win.at[i * SPAN + 1 + 2 * core + j], win.at[i * SPAN + (REACH + 1) * core + j],
+            ps.at[i * REACH + j], pr.at[i * REACH + j], partner, c,
         )
 
     def arrives(direction, k):
@@ -347,62 +363,111 @@
         held = c - (k - 1) >= 0 if direction > 0 else c + (k - 1) < col
         return held & beside[direction]
 
-    for d in (1, -1):
-        pl.when(sends(d, 1))(strip_to(d, 1).start)
+    def each(count, body):
+        def run(j, carry):
+            body(j)
+            return carry
+
+        lax.fori_loop(0, count, run, 0)
+
+    def pass_on(direction, k):
+        def row(j):
+            here = arrives(direction, k) & on_grid(REACH * core + j)
+
+            @pl.when(here)
+            def _():
+                hand_on(direction, k, j).wait_recv()
+
+            if k < REACH:
+                @pl.when(sends(direction, k + 1) & on_grid(REACH * core + j))
+                def _():
+                    hand_on(direction, k + 1, j).start()
+
+        each(REACH + 1, row)
+        i = REACH - direction * k
+
+        def across(j):
+            @pl.when(arrives(direction, k) & on_grid(1 + 2 * core + j))
+            def _():
+                share(i, j).start()
+
+        each(REACH, across)
+
+    def take_share(direction, k):
+        i = REACH - direction * k
+
+        def row(j):
+            @pl.when(arrives(direction, k) & on_grid((REACH + 1) * (1 - core) + j))
+            def _():
+                share(i, j).wait_recv()
+
+        each(REACH, row)
+
+    def far_strip(i):
+        total = None
+        for a in range(SPAN):
+            if abs(i - REACH) > 1 or abs(a - REACH) > 1:
+                term = dot(coup[order[0, i * SPAN + a]], win[i * SPAN + a])
+                total = term if total is None else total + term
+        far[...] += total
+
+    for d in within:
+        pl.when(within[-d])(far_wide(d).wait_recv)
+
+    def first_hand(j):
+        for d in (1, -1):
+            @pl.when(beside[d] & on_grid(REACH * core + j))
+            def _(d=d):
+                hand_on(d, 1, j).start()
+
+    each(REACH + 1, first_hand)
+
+    loads[2].wait()
+    wv[...] = dot(selfb[...], nb[4])
 
     for d in (-1, 1):
         pl.when(beside[d])(near_col(-d).wait_recv)
         for e in (-1, 1):
             pl.when(beside[d] & within[e])(near_to(e, d, 4 + d).start)
 
-    for k in range(1, REACH + 1):
-        for d in (1, -1):
-            pl.when(arrives(d, k))(strip_to(d, k).wait_recv)
-            if k < REACH:
-                pl.when(sends(d, k + 1))(strip_to(d, k + 1).start)
-            pl.when(arrives(d, k))(share(REACH - d * k).start)
-        if k == 1:
-            for e in (-1, 1):
-                for d in (-1, 0, 1):
-                    ok = within[-e] if d == 0 else within[-e] & beside[d]
-                    pl.when(ok)(near_to(e, d, 4 + d).wait_recv)
-            loads[3].wait()
-
-            def near_slot(s, carry):
-                cluster = near_ids[0, s]
-                place = (lax.div(cluster, col) - w + 1) * 3 + (lax.rem(cluster, col) - c + 1)
-                place = jnp.where(cluster >= 0, jnp.minimum(jnp.maximum(place, 0), 8), 9)
-
-                def near_rows(r, inner):
-                    piece = pl.ds(pl.multiple_of(r * step, step), step)
-                    wv[piece, :] += dot(near[s, piece, :], nb[place])
-                    return inner
-
-                return lax.fori_loop(0, rows // step, near_rows, carry)
-
-            lax.fori_loop(0, near_ids.shape[1], near_slot, 0)
-    for k in range(1, REACH + 1):
-        for d in (1, -1):
-            pl.when(arrives(d, k))(share(REACH - d * k).wait_recv)
     loads[4].wait()
+    coup[coup.shape[0] - 1] = jnp.zeros(coup.shape[1:], BF16)
     far[...] = jnp.zeros_like(far)
-
-    def far_slot(s, carry):
-        cluster = far_ids[0, s]
-        place = (lax.rem(cluster, col) - c + REACH) * SPAN + (lax.div(cluster, col) - w + REACH)
-        place = jnp.where(cluster >= 0, jnp.minimum(jnp.maximum(place, 0), SPAN * SPAN - 1), SPAN * SPAN)
-        far[...] += dot(coup[s], win[place])
-        return carry
-
-    lax.fori_loop(0, far_ids.shape[1], far_slot, 0)
-    far_b = far[...].astype(BF16)
-
-    def basis_part(k, carry):
-        piece = pl.ds(pl.multiple_of(k * step, step), step)
-        wv[piece, :] += dot(basis[piece, :], far_b)
-        return carry
-
-    lax.fori_loop(0, rows // step, basis_part, 0)
+    far_strip(REACH)
+    for d in (1, -1):
+        pass_on(d, 1)
+    for d in (1, -1):
+        take_share(d, 1)
+    far_strip(REACH - 1)
+    far_strip(REACH + 1)
+    for d in (1, -1):
+        pass_on(d, 2)
+
+    for e in (-1, 1):
+        for d in (-1, 0, 1):
+            ok = within[-e] if d == 0 else within[-e] & beside[d]
+            pl.when(ok)(near_to(e, d, 4 + d).wait_recv)
+    loads[3].wait()
+
+    def near_slot(s, carry):
+        cluster = near_ids[0, s]
+        place = (lax.div(cluster, col) - w + 1) * 3 + (lax.rem(cluster, col) - c + 1)
+        place = jnp.where(cluster >= 0, jnp.minimum(jnp.maximum(place, 0), 8), 9)
+        wv[...] += dot(near[s], nb[place])
+        return carry
+
+    lax.fori_loop(0, near_ids.shape[1], near_slot, 0)
+    for d in (1, -1):
+        pass_on(d, 3)
+    for d in (1, -1):
+        take_share(d, 2)
+    far_strip(REACH - 2)
+    far_strip(REACH + 2)
+    for d in (1, -1):
+        take_share(d, 3)
+    far_strip(REACH - 3)
+    far_strip(REACH + 3)
+    wv[...] += dot(basis[...], far[...].astype(BF16))
     local_grams([v, wv] if first else [vprev, x, wv], wv, g, step)
 
     pl.when(has_next)(to_next.wait_send)
@@ -418,8 +483,19 @@
         pl.when(within[d])(far_wide(d).wait_send)
     for k in range(1, REACH + 1):
         for d in (1, -1):
-            pl.when(sends(d, k))(strip_to(d, k).wait_send)
-            pl.when(arrives(d, k))(share(REACH - d * k).wait_send)
+
+            def sent(j, d=d, k=k):
+                @pl.when(sends(d, k) & on_grid(REACH * core + j))
+                def _():
+                    hand_on(d, k, j).wait_send()
+
+            def shared(j, d=d, k=k):
+                @pl.when(arrives(d, k) & on_grid(1 + 2 * core + j))
+                def _():
+                    share(REACH - d * k, j).wait_send()
+
+            each(REACH + 1, sent)
+            each(REACH, shared)
 
     all_reduce(w, c, wide, col, g, half, land, ysl, gram, send, recv)
 
@@ -454,7 +530,7 @@
         for i, a in enumerate(scaled):
             m = scratch[i]
             e = dot_full_t(dot_full(m, a), m) - eye
-            scratch[i] = m - dot_full(lower(e), m)
+            scratch[i] = m - dot_three(lower(e), m)
             error = error + jnp.sum(e * e)
         return step + 1, error
 
@@ -484,7 +560,27 @@
         scratch[i] = scratch[i] * by_lane
 
 
-def first_factor_kernel(g0, m, mt):
+def first_factor_kernel(col, far_ids, g0, m, mt, order):
+    w, c = lax.axis_index("wide"), lax.axis_index("col")
+    slots = far_ids.shape[1]
+
+    def clear(p, carry):
+        order[0, p] = slots
+        return carry
+
+    def put(s, carry):
+        cluster = far_ids[0, s]
+
+        @pl.when(cluster >= 0)
+        def _():
+            dc = lax.rem(cluster, col) - c + REACH
+            dw = lax.div(cluster, col) - w + REACH
+            order[0, dc * SPAN + dw] = s
+
+        return carry
+
+    lax.fori_loop(0, SPAN * SPAN, clear, 0)
+    lax.fori_loop(0, slots, put, 0)
     inverse_factors([g0[...]], m)
     mt[...] = m[0].T
 
@@ -500,20 +596,21 @@
 
 def last_kernel(step, g0, m0, gram1, mn, gram2, z1, z2, out, m):
     k = g0.shape[1]
-    beta = dot_full(m0[0], g0[...])
+    down = ((0,), (0,))
+    beta = dot_three(m0[0], g0[...])
     h1, h2 = gram1[0:k, :], gram2[0:k, :]
     n12, n22 = gram2[k : 2 * k, :], gram2[2 * k :, :]
     first = mn[1]
-    b1 = dot_full(first, t_dot_full(h1, beta))
+    b1 = dot_three(first, dot_three(h1, beta, down))
     t = dot_full(first, n12)
     inverse_factors([n22 - t_dot_full(t, t)], m)
-    b2 = t_dot_full(h2, beta) - t_dot_full(t, b1)
-    y2 = t_dot_full(m[0], dot_full(m[0], b2))
-    y1 = t_dot_full(first, b1 - dot_full(t, y2))
+    b2 = dot_three(h2, beta, down) - dot_three(t, b1, down)
+    y2 = dot_three(m[0], dot_three(m[0], b2), down)
+    y1 = dot_three(first, b1 - dot_three(t, y2), down)
 
     def combine(i, carry):
         piece = pl.ds(pl.multiple_of(i * step, step), step)
-        out[piece, :] = dot_full(z1[piece, :], y1) + dot_full(z2[piece, :], y2)
+        out[piece, :] = dot_three(z1[piece, :], y1) + dot_three(z2[piece, :], y2)
         return carry
 
     lax.fori_loop(0, out.shape[0] // step, combine, 0)
@@ -552,14 +649,14 @@
         compiler_params=talks(0),
         name="first_gram",
     )(rhs)
-    m0, mt0 = pl.pallas_call(
-        first_factor_kernel,
-        out_shape=(square, block(width)),
-        in_specs=[vmem],
-        out_specs=(vmem, vmem),
+    m0, mt0, listed = pl.pallas_call(
+        functools.partial(first_factor_kernel, col),
+        out_shape=(square, block(width), jax.ShapeDtypeStruct((1, SPAN * SPAN), jnp.int32)),
+        in_specs=[smem, vmem],
+        out_specs=(vmem, vmem, smem),
         compiler_params=local,
         name="first_factor",
-    )(gram0)
+    )(far_ids, gram0)
 
     def take_step(first, *blocks):
         grams = 2 if first else 3
@@ -576,7 +673,7 @@
                 pltpu.VMEM((rows, rank), BF16),
                 pltpu.VMEM((rows, rows), BF16),
                 pltpu.VMEM((slots, rows, rows), BF16),
-                pltpu.VMEM((links, rank, rank), BF16),
+                pltpu.VMEM((links + 1, rank, rank), BF16),
                 pltpu.VMEM((order, order), BF16),
                 pltpu.VMEM((2, margin, width), BF16),
                 pltpu.VMEM((order, width), BF16),
@@ -584,7 +681,7 @@
                 pltpu.VMEM((margin, width), F32),
                 pltpu.VMEM((2, margin, width), F32),
                 pltpu.VMEM((10, rows, width), BF16),
-                pltpu.VMEM((SPAN * SPAN + 1, rank, width), BF16),
+                pltpu.VMEM((SPAN * SPAN, rank, width), BF16),
                 pltpu.VMEM((rank, width), F32),
                 dma((5,)),
                 dma((4,)),
@@ -593,15 +690,15 @@
                 dma((9,)),
                 dma((SPAN,)),
                 dma((SPAN,)),
-                dma((SPAN,)),
-                dma((SPAN,)),
-                dma((SPAN,)),
-                dma((SPAN,)),
+                dma((SPAN * (REACH + 1),)),
+                dma((SPAN * (REACH + 1),)),
+                dma((SPAN * REACH,)),
+                dma((SPAN * REACH,)),
             ]
             + reduce_scratch(grams * width, width, wide, col),
             compiler_params=talks(1 if first else 2),
             name="first_step" if first else "second_step",
-        )(starts, near_ids, far_ids, *blocks, basis, self_block, near_block, couplings, schwarz_inverse)
+        )(starts, near_ids, listed, *blocks, basis, self_block, near_block, couplings, schwarz_inverse)
 
     v1, z1, w1, gram1 = take_step(True, rhs, mt0)
     m1, mt1, u = pl.pallas_call(

time: 345 us -> 319 us (0.925)
  Pallas kernels: 344 us -> 319 us
    pallas_call x2, Pallas kernels: 210 us -> 187 us  [take_step(): pl.pallas_call(functools.partial(step_kernel, wide, col, step, first), ou...]
where the time goes in v2:
time: 319 us
  Pallas kernels  319 us (100%)
    pallas_call x2, Pallas kernels, take_step(): pl.pallas_call(functools.partial(step_kernel, wide, col, step, first), ou...  187 us
    pallas_call x1, Pallas kernels, on_device(): pl.pallas_call(functools.partial(first_factor_kernel, col), out_shape=(sq...  87.8 us
    pallas_call x1, Pallas kernels, on_device(): pl.pallas_call(functools.partial(first_gram_kernel, wide, col, step), out...  27 us
    pallas_call x1, Pallas kernels, on_device(): pl.pallas_call(functools.partial(last_kernel, step), out_shape=block(rows...  9.92 us
    pallas_call x1, Pallas kernels, on_device(): pl.pallas_call(second_factor_kernel, out_shape=(jax.ShapeDtypeStruct((2,...  7.44 us

profile of v2, /device:TPU:1, one launch (start us, length us, event | category | flops | bytes accessed | tf_op | source)
XLA Modules:
  0.0 319.1 jit_solution(14339335661857274080)
XLA Ops:
  0.0 27.0 %first_gram.1.g0 = f32[256,256]{1,0:T(8,128)} custom-call(f32[768,256]{1,0:T(8,128)} %refs_3_.1), custom_call_target="tpu_custom_call" | custom-call | tf_op jit(solution)/shard_map/first_gram/pallas_call | solution.py:643
  27.0 87.8 %first_factor.1 = (f32[1,256,256]{2,1,0:T(8,128)}, f32[256,256]{1,0:T(8,128)}, s32[1,49]{1,0:T(1,128)}) custom-call(s32[1,40]{1,0:T(1,128)} %far_ids.1, f32[256,256]{1,0:T(8,128)} %first_gram.1.g0), custom_call_target="tpu_custom_call" | custom-call | tf_op jit(solution)/shard_map/first_factor/pallas_call | solution.py:652
  114.8 91.8 %first_step.1 = (f32[768,256]{1,0:T(8,128)}, f32[768,256]{1,0:T(8,128)}, f32[768,256]{1,0:T(8,128)}, f32[512,256]{1,0:T(8,128)}) custom-call(s32[1,2]{1,0:T(1,128)} %refs_0_.3, s32[1,8]{1,0:T(1,128)} %refs_1_.3, s32[1,49]{1,0:T(1,128)} %get-tuple-element.18.refs_2_, f32[768,256]{1,0:T(8,128)} %refs_3_.1, f32[256,256]{1,0:T(8,128)} %get-tuple-element.19.refs_4_, ...), custom_call_target="tpu_custom_call" | custom-call | tf_op jit(solution)/shard_map/first_step/pallas_call | solution.py:666
  206.5 7.4 %second_factor.1 = (f32[2,256,256]{2,1,0:T(8,128)}, f32[256,256]{1,0:T(8,128)}, f32[256,256]{1,0:T(8,128)}) custom-call(f32[512,256]{1,0:T(8,128)} %get-tuple-element.20.gram.gram1), custom_call_target="tpu_custom_call" | custom-call | tf_op jit(solution)/shard_map/second_factor/pallas_call | solution.py:704
  214.0 95.2 %second_step.1 = (f32[768,256]{1,0:T(8,128)}, f32[768,256]{1,0:T(8,128)}) custom-call(s32[1,2]{1,0:T(1,128)} %refs_0_.3, s32[1,8]{1,0:T(1,128)} %refs_1_.3, s32[1,49]{1,0:T(1,128)} %get-tuple-element.18.refs_2_, f32[768,256]{1,0:T(8,128)} %get-tuple-element.22.refs_3_, f32[256,256]{1,0:T(8,128)} %get-tuple-element.23.refs_4_, ...), custom_call_target="tpu_custom_call" | custom-call | tf_op jit(solution)/shard_map/second_step/pallas_call | solution.py:666
  309.1 9.9 %last.1 = f32[768,256]{1,0:T(8,128)} custom-call(f32[256,256]{1,0:T(8,128)} %first_gram.1.g0, f32[1,256,256]{2,1,0:T(8,128)} %get-tuple-element.17.m0, f32[512,256]{1,0:T(8,128)} %get-tuple-element.20.gram.gram1, f32[2,256,256]{2,1,0:T(8,128)} %get-tuple-element.21.mn, f32[768,256]{1,0:T(8,128)} %get-tuple-element.26.gram2, ...), custom_call_target="tpu_custom_call" | custom-call | tf_op jit(solution)/shard_map/last/pallas_call | solution.py:713

commit v3 on v2

--- a/solution.py
+++ b/solution.py
@@ -213,7 +213,7 @@
         (starts, near_ids, order, x, mt, vprev, u, basis_h, self_h, near_h, coup_h, sch_h, *rest) = refs
         (z, gram, v, wv, *rest) = rest
     (basis, selfb, near, coup, sch, stage, dom, pad_next, pad_prev, edge, nb, win, far, *rest) = rest
-    (load, hs, hr, ns, nr, ws, wr, rs, rr, ps, pr, *reduce) = rest
+    (load, hs, hr, ns, nr, ws, wr, rs, rr, es, ps, pr, *reduce) = rest
     g, half, land, ysl, send, recv = reduce
     w, c = lax.axis_index("wide"), lax.axis_index("col")
     core = lax.rem(w, 2)
@@ -350,6 +350,32 @@
             rs.at[lands * (REACH + 1) + j], rr.at[lands * (REACH + 1) + j], w, c + direction,
         )
 
+    def jump(direction, j):
+        lands = REACH - direction * REACH
+        a = REACH * core + j
+        return remote(
+            win.at[(REACH + direction) * SPAN + a], win.at[lands * SPAN + a],
+            rs.at[lands * (REACH + 1) + j], rr.at[lands * (REACH + 1) + j],
+            w, c + direction * (REACH + 1),
+        )
+
+    def jumps(direction):
+        return c + REACH + 1 < col if direction > 0 else c - REACH - 1 >= 0
+
+    def from_end(direction, j):
+        lands = REACH - direction * REACH
+        a = REACH * core + j
+        return remote(
+            win.at[REACH * SPAN + a], win.at[lands * SPAN + a],
+            es.at[lands * (REACH + 1) + j], rr.at[lands * (REACH + 1) + j],
+            w, c + direction * REACH,
+        )
+
+    def at_end(direction):
+        if direction > 0:
+            return (c == 0) & (c + REACH < col)
+        return (c == col - 1) & (c - REACH >= 0)
+
     def share(i, j):
         return remote(
             win.at[i * SPAN + 1 + 2 * core + j], win.at[i * SPAN + (REACH + 1) * core + j],
@@ -378,7 +404,12 @@
             def _():
                 hand_on(direction, k, j).wait_recv()
 
-            if k < REACH:
+            if k == 1:
+                @pl.when(here & jumps(-direction))
+                def _():
+                    jump(-direction, j).start()
+
+            if k + 1 < REACH:
                 @pl.when(sends(direction, k + 1) & on_grid(REACH * core + j))
                 def _():
                     hand_on(direction, k + 1, j).start()
@@ -419,6 +450,10 @@
             @pl.when(beside[d] & on_grid(REACH * core + j))
             def _(d=d):
                 hand_on(d, 1, j).start()
+
+            @pl.when(at_end(d) & on_grid(REACH * core + j))
+            def _(d=d):
+                from_end(d, j).start()
 
     each(REACH + 1, first_hand)
 
@@ -485,9 +520,18 @@
         for d in (1, -1):
 
             def sent(j, d=d, k=k):
-                @pl.when(sends(d, k) & on_grid(REACH * core + j))
-                def _():
-                    hand_on(d, k, j).wait_send()
+                if k < REACH:
+                    @pl.when(sends(d, k) & on_grid(REACH * core + j))
+                    def _():
+                        hand_on(d, k, j).wait_send()
+                else:
+                    @pl.when(arrives(-d, 1) & jumps(d) & on_grid(REACH * core + j))
+                    def _():
+                        jump(d, j).wait_send()
+
+                    @pl.when(at_end(d) & on_grid(REACH * core + j))
+                    def _():
+                        from_end(d, j).wait_send()
 
             def shared(j, d=d, k=k):
                 @pl.when(arrives(d, k) & on_grid(1 + 2 * core + j))
@@ -692,6 +736,7 @@
                 dma((SPAN,)),
                 dma((SPAN * (REACH + 1),)),
                 dma((SPAN * (REACH + 1),)),
+                dma((SPAN * (REACH + 1),)),
                 dma((SPAN * REACH,)),
                 dma((SPAN * REACH,)),
             ]

time: 319 us -> 315 us (0.987)
  Pallas kernels: 319 us -> 315 us
    pallas_call x2, Pallas kernels: 187 us -> 183 us  [take_step(): pl.pallas_call(functools.partial(step_kernel, wide, col, step, first), ou...]
where the time goes in v3:
time: 315 us
  Pallas kernels  315 us (100%)
    pallas_call x2, Pallas kernels, take_step(): pl.pallas_call(functools.partial(step_kernel, wide, col, step, first), ou...  183 us
    pallas_call x1, Pallas kernels, on_device(): pl.pallas_call(functools.partial(first_factor_kernel, col), out_shape=(sq...  87.8 us
    pallas_call x1, Pallas kernels, on_device(): pl.pallas_call(functools.partial(first_gram_kernel, wide, col, step), out...  27 us
    pallas_call x1, Pallas kernels, on_device(): pl.pallas_call(functools.partial(last_kernel, step), out_shape=block(rows...  9.93 us
    pallas_call x1, Pallas kernels, on_device(): pl.pallas_call(second_factor_kernel, out_shape=(jax.ShapeDtypeStruct((2,...  7.43 us

profile of v3, /device:TPU:1, one launch (start us, length us, event | category | flops | bytes accessed | tf_op | source)
XLA Modules:
  0.0 314.9 jit_solution(17466098884382311421)
XLA Ops:
  0.0 27.0 %first_gram.1.g0 = f32[256,256]{1,0:T(8,128)} custom-call(f32[768,256]{1,0:T(8,128)} %refs_3_.1), custom_call_target="tpu_custom_call" | custom-call | tf_op jit(solution)/shard_map/first_gram/pallas_call | solution.py:687
  27.0 87.8 %first_factor.1 = (f32[1,256,256]{2,1,0:T(8,128)}, f32[256,256]{1,0:T(8,128)}, s32[1,49]{1,0:T(1,128)}) custom-call(s32[1,40]{1,0:T(1,128)} %far_ids.1, f32[256,256]{1,0:T(8,128)} %first_gram.1.g0), custom_call_target="tpu_custom_call" | custom-call | tf_op jit(solution)/shard_map/first_factor/pallas_call | solution.py:696
  114.8 89.8 %first_step.1 = (f32[768,256]{1,0:T(8,128)}, f32[768,256]{1,0:T(8,128)}, f32[768,256]{1,0:T(8,128)}, f32[512,256]{1,0:T(8,128)}) custom-call(s32[1,2]{1,0:T(1,128)} %refs_0_.3, s32[1,8]{1,0:T(1,128)} %refs_1_.3, s32[1,49]{1,0:T(1,128)} %get-tuple-element.18.refs_2_, f32[768,256]{1,0:T(8,128)} %refs_3_.1, f32[256,256]{1,0:T(8,128)} %get-tuple-element.19.refs_4_, ...), custom_call_target="tpu_custom_call" | custom-call | tf_op jit(solution)/shard_map/first_step/pallas_call | solution.py:710
  204.6 7.4 %second_factor.1 = (f32[2,256,256]{2,1,0:T(8,128)}, f32[256,256]{1,0:T(8,128)}, f32[256,256]{1,0:T(8,128)}) custom-call(f32[512,256]{1,0:T(8,128)} %get-tuple-element.20.gram.gram1), custom_call_target="tpu_custom_call" | custom-call | tf_op jit(solution)/shard_map/second_factor/pallas_call | solution.py:749
  212.0 93.0 %second_step.1 = (f32[768,256]{1,0:T(8,128)}, f32[768,256]{1,0:T(8,128)}) custom-call(s32[1,2]{1,0:T(1,128)} %refs_0_.3, s32[1,8]{1,0:T(1,128)} %refs_1_.3, s32[1,49]{1,0:T(1,128)} %get-tuple-element.18.refs_2_, f32[768,256]{1,0:T(8,128)} %get-tuple-element.22.refs_3_, f32[256,256]{1,0:T(8,128)} %get-tuple-element.23.refs_4_, ...), custom_call_target="tpu_custom_call" | custom-call | tf_op jit(solution)/shard_map/second_step/pallas_call | solution.py:710
  305.0 9.9 %last.1 = f32[768,256]{1,0:T(8,128)} custom-call(f32[256,256]{1,0:T(8,128)} %first_gram.1.g0, f32[1,256,256]{2,1,0:T(8,128)} %get-tuple-element.17.m0, f32[512,256]{1,0:T(8,128)} %get-tuple-element.20.gram.gram1, f32[2,256,256]{2,1,0:T(8,128)} %get-tuple-element.21.mn, f32[768,256]{1,0:T(8,128)} %get-tuple-element.26.gram2, ...), custom_call_target="tpu_custom_call" | custom-call | tf_op jit(solution)/shard_map/last/pallas_call | solution.py:758

commit v4 on v3

--- a/solution.py
+++ b/solution.py
@@ -197,20 +197,53 @@
         lax.fori_loop(1, rows // step, add, 0)
 
 
-def first_gram_kernel(wide, col, step, rhs, out, g, half, land, ysl, send, recv):
+def clear_ends(halo, c, col):
+    for i, end in ((0, 0), (1, col - 1)):
+
+        @pl.when(c == end)
+        def _(i=i):
+            halo[i] = jnp.zeros(halo.shape[1:], F32)
+
+
+def pick_rows(starts, block, stage):
+    margin, rows = stage.shape[1], block.shape[0]
+    for i in range(2):
+        chosen = picks(starts[0, 1 - i], margin, rows)
+        high, mid, low = three_parts(block[...])
+        stage[i] = (dot(chosen, low) + dot(chosen, mid)) + dot(chosen, high)
+
+
+def halo_copies(stage, halo, send, recv, w, c, col):
+    return (
+        (c < col - 1, c > 0, remote(stage.at[0], halo.at[0], send.at[0], recv.at[0], w, c + 1)),
+        (c > 0, c < col - 1, remote(stage.at[1], halo.at[1], send.at[1], recv.at[1], w, c - 1)),
+    )
+
+
+def first_gram_kernel(
+    wide, col, step, starts, rhs, out, halo, stage, hs, hr, g, half, land, ysl, send, recv
+):
     w, c = lax.axis_index("wide"), lax.axis_index("col")
+    clear_ends(halo, c, col)
     greet(w, c, wide, col)
     local_grams([rhs], rhs, g, step)
+    pick_rows(starts, rhs, stage)
     meet(wide, col)
+    copies = halo_copies(stage, halo, hs, hr, w, c, col)
+    for sends, _, copy in copies:
+        pl.when(sends)(copy.start)
     all_reduce(w, c, wide, col, g, half, land, ysl, out, send, recv)
+    for sends, takes, copy in copies:
+        pl.when(sends)(copy.wait_send)
+        pl.when(takes)(copy.wait_recv)
 
 
 def step_kernel(wide, col, step, first, *refs):
     if first:
-        (starts, near_ids, order, x, mt, basis_h, self_h, near_h, coup_h, sch_h, *rest) = refs
-        (v, z, wv, gram, *rest) = rest
+        (starts, near_ids, order, x, mt, halo_x, basis_h, self_h, near_h, coup_h, sch_h, *rest) = refs
+        (v, z, wv, halo_v, halo_w, gram, *rest) = rest
     else:
-        (starts, near_ids, order, x, mt, vprev, u, basis_h, self_h, near_h, coup_h, sch_h, *rest) = refs
+        (starts, near_ids, order, x, mt, halo_x, vprev, u, halo_vprev, basis_h, self_h, near_h, coup_h, sch_h, *rest) = refs
         (z, gram, v, wv, *rest) = rest
     (basis, selfb, near, coup, sch, stage, dom, pad_next, pad_prev, edge, nb, win, far, *rest) = rest
     (load, hs, hr, ns, nr, ws, wr, rs, rr, es, ps, pr, *reduce) = rest
@@ -236,12 +269,10 @@
 
     @pl.when(jnp.logical_not(has_prev))
     def _():
-        dom[0:margin, :] = jnp.zeros((margin, width), BF16)
         pad_prev[...] = jnp.zeros((margin, width), F32)
 
     @pl.when(jnp.logical_not(has_next))
     def _():
-        dom[margin + rows :, :] = jnp.zeros((margin, width), BF16)
         pad_next[...] = jnp.zeros((margin, width), F32)
 
     for i in range(SPAN):
@@ -254,6 +285,8 @@
                 def _(cell=i * SPAN + a):
                     win[cell] = jnp.zeros(win.shape[1:], BF16)
 
+    if first:
+        clear_ends(halo_w, c, col)
     greet(w, c, wide, col)
 
     def make_v(k, carry):
@@ -267,29 +300,25 @@
 
     lax.fori_loop(0, rows // step, make_v, 0)
     start_prev, start_next = starts[0, 0], starts[0, 1]
-    stage[0] = dot(picks(start_next, margin, rows), dom[margin : margin + rows, :]).astype(BF16)
-    stage[1] = dot(picks(start_prev, margin, rows), dom[margin : margin + rows, :]).astype(BF16)
-    meet(wide, col)
-
-    to_next = remote(stage.at[0], dom.at[pl.ds(0, margin)], hs.at[0], hr.at[0], w, c + 1)
-    to_prev = remote(
-        stage.at[1], dom.at[pl.ds(margin + rows, margin)], hs.at[1], hr.at[1], w, c - 1
-    )
+    for i, place in ((0, 0), (1, margin + rows)):
+        value = dot_full(halo_x[i], mt[...])
+        if first:
+            halo_v[i] = value
+        else:
+            value += dot_full(halo_vprev[i], u[...])
+        dom[place : place + margin, :] = value.astype(BF16)
+
     out_prev = remote(
         edge.at[0], pad_next, hs.at[2], hr.at[2], w, c - 1
     )
     out_next = remote(
         edge.at[1], pad_prev, hs.at[3], hr.at[3], w, c + 1
     )
-    pl.when(has_next)(to_next.start)
-    pl.when(has_prev)(to_prev.start)
-
     nb[9] = jnp.zeros((rows, width), BF16)
 
     loads[0].wait()
-    pl.when(has_prev)(to_next.wait_recv)
-    pl.when(has_next)(to_prev.wait_recv)
     edge[0] = dot(sch[0:margin, :], dom[...])
+    meet(wide, col)
     pl.when(has_prev)(out_prev.start)
     edge[1] = dot(sch[margin + rows :, :], dom[...])
     pl.when(has_next)(out_next.start)
@@ -322,9 +351,6 @@
     within = {d: (w + d >= 0) & (w + d < wide) for d in range(-REACH, REACH + 1) if d}
     for d in (-1, 1):
         pl.when(beside[d])(near_col(d).start)
-    for d in (-1, 1):
-        pl.when(within[d])(near_to(d, 0, 4).start)
-
     centre = REACH * SPAN + REACH
     win[centre] = lax.dot_general(
         basis[...], nb[4], (((0,), (0,)), ((), ())), preferred_element_type=F32
@@ -337,6 +363,8 @@
 
     for d in (1, -1, 2, -2, 3, -3):
         pl.when(within[d])(far_wide(d).start)
+    for d in (-1, 1):
+        pl.when(within[d])(near_to(d, 0, 4).start)
 
     def on_grid(a):
         return (w + a - REACH >= 0) & (w + a - REACH < wide)
@@ -475,9 +503,6 @@
         take_share(d, 1)
     far_strip(REACH - 1)
     far_strip(REACH + 1)
-    for d in (1, -1):
-        pass_on(d, 2)
-
     for e in (-1, 1):
         for d in (-1, 0, 1):
             ok = within[-e] if d == 0 else within[-e] & beside[d]
@@ -493,6 +518,7 @@
 
     lax.fori_loop(0, near_ids.shape[1], near_slot, 0)
     for d in (1, -1):
+        pass_on(d, 2)
         pass_on(d, 3)
     for d in (1, -1):
         take_share(d, 2)
@@ -503,10 +529,13 @@
     far_strip(REACH - 3)
     far_strip(REACH + 3)
     wv[...] += dot(basis[...], far[...].astype(BF16))
+    if first:
+        pick_rows(starts, wv, stage)
+        copies = halo_copies(stage, halo_w, hs, hr, w, c, col)
+        for goes, _, copy in copies:
+            pl.when(goes)(copy.start)
     local_grams([v, wv] if first else [vprev, x, wv], wv, g, step)
 
-    pl.when(has_next)(to_next.wait_send)
-    pl.when(has_prev)(to_prev.wait_send)
     pl.when(has_prev)(out_prev.wait_send)
     pl.when(has_next)(out_next.wait_send)
     for d in (-1, 1):
@@ -542,6 +571,10 @@
             each(REACH, shared)
 
     all_reduce(w, c, wide, col, g, half, land, ysl, gram, send, recv)
+    if first:
+        for goes, takes, copy in copies:
+            pl.when(goes)(copy.wait_send)
+            pl.when(takes)(copy.wait_recv)
 
 
 def inverse_factors(matrices, scratch):
@@ -684,15 +717,21 @@
             collective_id=number, has_side_effects=True, vmem_limit_bytes=VMEM_BYTES
         )
 
-    gram0 = pl.pallas_call(
+    halo = jax.ShapeDtypeStruct((2, margin, width), F32)
+    gram0, halo_x = pl.pallas_call(
         functools.partial(first_gram_kernel, wide, col, step),
-        out_shape=block(width),
-        in_specs=[vmem],
-        out_specs=vmem,
-        scratch_shapes=reduce_scratch(width, width, wide, col),
+        out_shape=(block(width), halo),
+        in_specs=[smem, vmem],
+        out_specs=(vmem, vmem),
+        scratch_shapes=[
+            pltpu.VMEM((2, margin, width), F32),
+            pltpu.SemaphoreType.DMA((2,)),
+            pltpu.SemaphoreType.DMA((2,)),
+        ]
+        + reduce_scratch(width, width, wide, col),
         compiler_params=talks(0),
         name="first_gram",
-    )(rhs)
+    )(starts, rhs)
     m0, mt0, listed = pl.pallas_call(
         functools.partial(first_factor_kernel, col),
         out_shape=(square, block(width), jax.ShapeDtypeStruct((1, SPAN * SPAN), jnp.int32)),
@@ -704,7 +743,7 @@
 
     def take_step(first, *blocks):
         grams = 2 if first else 3
-        outs = [block(rows)] * 3 if first else [block(rows)]
+        outs = [block(rows)] * 3 + [halo] * 2 if first else [block(rows)]
         held = [] if first else [pltpu.VMEM((rows, width), F32)] * 2
         dma = pltpu.SemaphoreType.DMA
         return pl.pallas_call(
@@ -719,7 +758,7 @@
                 pltpu.VMEM((slots, rows, rows), BF16),
                 pltpu.VMEM((links + 1, rank, rank), BF16),
                 pltpu.VMEM((order, order), BF16),
-                pltpu.VMEM((2, margin, width), BF16),
+                pltpu.VMEM((2, margin, width), F32),
                 pltpu.VMEM((order, width), BF16),
                 pltpu.VMEM((margin, width), F32),
                 pltpu.VMEM((margin, width), F32),
@@ -745,7 +784,7 @@
             name="first_step" if first else "second_step",
         )(starts, near_ids, listed, *blocks, basis, self_block, near_block, couplings, schwarz_inverse)
 
-    v1, z1, w1, gram1 = take_step(True, rhs, mt0)
+    v1, z1, w1, halo_v, halo_w, gram1 = take_step(True, rhs, mt0, halo_x)
     m1, mt1, u = pl.pallas_call(
         second_factor_kernel,
         out_shape=(jax.ShapeDtypeStruct((2, width, width), F32), block(width), block(width)),
@@ -754,7 +793,7 @@
         compiler_params=local,
         name="second_factor",
     )(gram1)
-    z2, gram2 = take_step(False, w1, mt1, v1, u)
+    z2, gram2 = take_step(False, w1, mt1, halo_w, v1, u, halo_v)
     return pl.pallas_call(
         functools.partial(last_kernel, step),
         out_shape=block(rows),

time: 315 us -> 311 us (0.987)
  Pallas kernels: 315 us -> 310 us
    pallas_call x2, Pallas kernels: 183 us -> 174 us  [take_step(): pl.pallas_call(functools.partial(step_kernel, wide, col, step, first), ou...]
    pallas_call x1, Pallas kernels: 27 us -> 31 us  [on_device(): pl.pallas_call(functools.partial(first_gram_kernel, wide, col, step), out...]
where the time goes in v4:
time: 311 us; the launch traced here: 310 us
  Pallas kernels  310 us (100%)
    pallas_call x2, Pallas kernels, take_step(): pl.pallas_call(functools.partial(step_kernel, wide, col, step, first), ou...  174 us
    pallas_call x1, Pallas kernels, on_device(): pl.pallas_call(functools.partial(first_factor_kernel, col), out_shape=(sq...  87.8 us
    pallas_call x1, Pallas kernels, on_device(): pl.pallas_call(functools.partial(first_gram_kernel, wide, col, step), out...  31 us
    pallas_call x1, Pallas kernels, on_device(): pl.pallas_call(functools.partial(last_kernel, step), out_shape=block(rows...  9.92 us
    pallas_call x1, Pallas kernels, on_device(): pl.pallas_call(second_factor_kernel, out_shape=(jax.ShapeDtypeStruct((2,...  7.25 us

profile of v4, /device:TPU:1, one launch (start us, length us, event | category | flops | bytes accessed | tf_op | source)
XLA Modules:
  0.0 310.4 jit_solution(15988812040399461736)
XLA Ops:
  0.0 31.0 %first_gram.1 = (f32[256,256]{1,0:T(8,128)}, f32[2,256,256]{2,1,0:T(8,128)}) custom-call(s32[1,2]{1,0:T(1,128)} %refs_0_.3, f32[768,256]{1,0:T(8,128)} %refs_3_.1), custom_call_target="tpu_custom_call" | custom-call | tf_op jit(solution)/shard_map/first_gram/pallas_call | solution.py:721
  31.1 87.8 %first_factor.1 = (f32[1,256,256]{2,1,0:T(8,128)}, f32[256,256]{1,0:T(8,128)}, s32[1,49]{1,0:T(1,128)}) custom-call(s32[1,40]{1,0:T(1,128)} %far_ids.1, f32[256,256]{1,0:T(8,128)} %get-tuple-element.21.g0), custom_call_target="tpu_custom_call" | custom-call | tf_op jit(solution)/shard_map/first_factor/pallas_call | solution.py:735
  118.8 87.0 %first_step.1 = (f32[768,256]{1,0:T(8,128)}, f32[768,256]{1,0:T(8,128)}, f32[768,256]{1,0:T(8,128)}, f32[2,256,256]{2,1,0:T(8,128)}, f32[2,256,256]{2,1,0:T(8,128)}, /*index=5*/f32[512,256]{1,0:T(8,128)}) custom-call(s32[1,2]{1,0:T(1,128)} %refs_0_.3, s32[1,8]{1,0:T(1,128)} %refs_1_.3, s32[1,49]{1,0:T(1,128)} %get-tuple-element.23.refs_2_, ...), custom_call_target="tpu_custom_call" | custom-call | tf_op jit(solution)/shard_map/first_step/pallas_call | solution.py:749
  205.9 7.2 %second_factor.1 = (f32[2,256,256]{2,1,0:T(8,128)}, f32[256,256]{1,0:T(8,128)}, f32[256,256]{1,0:T(8,128)}) custom-call(f32[512,256]{1,0:T(8,128)} %get-tuple-element.26.gram.gram1), custom_call_target="tpu_custom_call" | custom-call | tf_op jit(solution)/shard_map/second_factor/pallas_call | solution.py:788
  213.1 87.3 %second_step.1 = (f32[768,256]{1,0:T(8,128)}, f32[768,256]{1,0:T(8,128)}) custom-call(s32[1,2]{1,0:T(1,128)} %refs_0_.3, s32[1,8]{1,0:T(1,128)} %refs_1_.3, s32[1,49]{1,0:T(1,128)} %get-tuple-element.23.refs_2_, f32[768,256]{1,0:T(8,128)} %get-tuple-element.28.refs_3_, f32[256,256]{1,0:T(8,128)} %get-tuple-element.29.refs_4_, ...), custom_call_target="tpu_custom_call" | custom-call | tf_op jit(solution)/shard_map/second_step/pallas_call | solution.py:749
  300.5 9.9 %last.1 = f32[768,256]{1,0:T(8,128)} custom-call(f32[256,256]{1,0:T(8,128)} %get-tuple-element.21.g0, f32[1,256,256]{2,1,0:T(8,128)} %get-tuple-element.22.m0, f32[512,256]{1,0:T(8,128)} %get-tuple-element.26.gram.gram1, f32[2,256,256]{2,1,0:T(8,128)} %get-tuple-element.27.mn, f32[768,256]{1,0:T(8,128)} %get-tuple-element.34.gram2, ...), custom_call_target="tpu_custom_call" | custom-call | tf_op jit(solution)/shard_map/last/pallas_call | solution.py:797

commit v5 on v4

--- a/solution.py
+++ b/solution.py
@@ -104,7 +104,7 @@
     pl.semaphore_wait(pltpu.get_barrier_semaphore(), wide + col - 2)
 
 
-def all_reduce(w, c, wide, col, g, half, land, ysl, out, send, recv):
+def all_reduce(w, c, wide, col, g, half, land, ysl, out, send, recv, others=()):
     rows = g.shape[0]
     high = rows // 2
     part = high // col
@@ -134,6 +134,8 @@
         return carry
 
     lax.fori_loop(1, col, scatter, 0)
+    for goes, _, copy in others:
+        pl.when(goes)(copy.start)
     many = (col - 1) * part
     remote(g.at[pl.ds(0, many)], land, send.at[1], recv.at[1], w, c).wait()
     total = g[pl.ds(own, part), :]
@@ -167,6 +169,9 @@
     swap = remote(out.at[spot], out.at[spot], send.at[4], recv.at[4], partner, c)
     swap.start()
     swap.wait()
+    for goes, takes, copy in others:
+        pl.when(goes)(copy.wait_send)
+        pl.when(takes)(copy.wait_recv)
 
 
 def reduce_scratch(rows, width, wide, col):
@@ -182,19 +187,10 @@
     ]
 
 
-def local_grams(lefts, right, g, step):
+def local_grams(lefts, right, g):
     width = right.shape[1]
-    rows = right.shape[0]
     for i, left in enumerate(lefts):
-        spot = slice(i * width, (i + 1) * width)
-        g[spot, :] = dot_three(left[0:step, :], right[0:step, :], ((0,), (0,)))
-
-        def add(k, carry, left=left, spot=spot):
-            piece = pl.ds(pl.multiple_of(k * step, step), step)
-            g[spot, :] += dot_three(left[piece, :], right[piece, :], ((0,), (0,)))
-            return carry
-
-        lax.fori_loop(1, rows // step, add, 0)
+        g[i * width : (i + 1) * width, :] = dot_three(left[...], right[...], ((0,), (0,)))
 
 
 def clear_ends(halo, c, col):
@@ -226,16 +222,11 @@
     w, c = lax.axis_index("wide"), lax.axis_index("col")
     clear_ends(halo, c, col)
     greet(w, c, wide, col)
-    local_grams([rhs], rhs, g, step)
+    local_grams([rhs], rhs, g)
     pick_rows(starts, rhs, stage)
     meet(wide, col)
     copies = halo_copies(stage, halo, hs, hr, w, c, col)
-    for sends, _, copy in copies:
-        pl.when(sends)(copy.start)
-    all_reduce(w, c, wide, col, g, half, land, ysl, out, send, recv)
-    for sends, takes, copy in copies:
-        pl.when(sends)(copy.wait_send)
-        pl.when(takes)(copy.wait_recv)
+    all_reduce(w, c, wide, col, g, half, land, ysl, out, send, recv, copies)
 
 
 def step_kernel(wide, col, step, first, *refs):
@@ -509,14 +500,19 @@
             pl.when(ok)(near_to(e, d, 4 + d).wait_recv)
     loads[3].wait()
 
-    def near_slot(s, carry):
-        cluster = near_ids[0, s]
+    at = []
+    for slot in range(near_ids.shape[1]):
+        cluster = near_ids[0, slot]
         place = (lax.div(cluster, col) - w + 1) * 3 + (lax.rem(cluster, col) - c + 1)
-        place = jnp.where(cluster >= 0, jnp.minimum(jnp.maximum(place, 0), 8), 9)
-        wv[...] += dot(near[s], nb[place])
-        return carry
-
-    lax.fori_loop(0, near_ids.shape[1], near_slot, 0)
+        at.append(jnp.where(cluster >= 0, jnp.minimum(jnp.maximum(place, 0), 8), 9))
+    for k in range(rows // step):
+        piece = slice(k * step, (k + 1) * step)
+        total = None
+        for slot, place in enumerate(at):
+            term = dot(near[slot, piece, :], nb[place])
+            total = term if total is None else total + term
+        wv[piece, :] += total
+
     for d in (1, -1):
         pass_on(d, 2)
         pass_on(d, 3)
@@ -531,10 +527,7 @@
     wv[...] += dot(basis[...], far[...].astype(BF16))
     if first:
         pick_rows(starts, wv, stage)
-        copies = halo_copies(stage, halo_w, hs, hr, w, c, col)
-        for goes, _, copy in copies:
-            pl.when(goes)(copy.start)
-    local_grams([v, wv] if first else [vprev, x, wv], wv, g, step)
+    local_grams([v, wv] if first else [vprev, x, wv], wv, g)
 
     pl.when(has_prev)(out_prev.wait_send)
     pl.when(has_next)(out_next.wait_send)
@@ -570,11 +563,8 @@
             each(REACH + 1, sent)
             each(REACH, shared)
 
-    all_reduce(w, c, wide, col, g, half, land, ysl, gram, send, recv)
-    if first:
-        for goes, takes, copy in copies:
-            pl.when(goes)(copy.wait_send)
-            pl.when(takes)(copy.wait_recv)
+    copies = halo_copies(stage, halo_w, hs, hr, w, c, col) if first else ()
+    all_reduce(w, c, wide, col, g, half, land, ysl, gram, send, recv, copies)
 
 
 def inverse_factors(matrices, scratch):

time: 311 us -> 311 us (level)
  no operation moved by 1% of the time
where the time goes in v5:
time: 311 us
  Pallas kernels  311 us (100%)
    pallas_call x2, Pallas kernels, take_step(): pl.pallas_call(functools.partial(step_kernel, wide, col, step, first), ou...  177 us
    pallas_call x1, Pallas kernels, on_device(): pl.pallas_call(functools.partial(first_factor_kernel, col), out_shape=(sq...  87.8 us
    pallas_call x1, Pallas kernels, on_device(): pl.pallas_call(functools.partial(first_gram_kernel, wide, col, step), out...  28.2 us
    pallas_call x1, Pallas kernels, on_device(): pl.pallas_call(functools.partial(last_kernel, step), out_shape=block(rows...  10.2 us
    pallas_call x1, Pallas kernels, on_device(): pl.pallas_call(second_factor_kernel, out_shape=(jax.ShapeDtypeStruct((2,...  7.46 us

profile of v5, /device:TPU:1, one launch (start us, length us, event | category | flops | bytes accessed | tf_op | source)
XLA Modules:
  0.0 310.5 jit_solution(8976221245955624069)
XLA Ops:
  0.0 28.2 %first_gram.1 = (f32[256,256]{1,0:T(8,128)}, f32[2,256,256]{2,1,0:T(8,128)}) custom-call(s32[1,2]{1,0:T(1,128)} %refs_0_.3, f32[768,256]{1,0:T(8,128)} %refs_3_.1), custom_call_target="tpu_custom_call" | custom-call | tf_op jit(solution)/shard_map/first_gram/pallas_call | solution.py:711
  28.2 87.8 %first_factor.1 = (f32[1,256,256]{2,1,0:T(8,128)}, f32[256,256]{1,0:T(8,128)}, s32[1,49]{1,0:T(1,128)}) custom-call(s32[1,40]{1,0:T(1,128)} %far_ids.1, f32[256,256]{1,0:T(8,128)} %get-tuple-element.21.g0), custom_call_target="tpu_custom_call" | custom-call | tf_op jit(solution)/shard_map/first_factor/pallas_call | solution.py:725
  116.0 88.5 %first_step.1 = (f32[768,256]{1,0:T(8,128)}, f32[768,256]{1,0:T(8,128)}, f32[768,256]{1,0:T(8,128)}, f32[2,256,256]{2,1,0:T(8,128)}, f32[2,256,256]{2,1,0:T(8,128)}, /*index=5*/f32[512,256]{1,0:T(8,128)}) custom-call(s32[1,2]{1,0:T(1,128)} %refs_0_.3, s32[1,8]{1,0:T(1,128)} %refs_1_.3, s32[1,49]{1,0:T(1,128)} %get-tuple-element.23.refs_2_, ...), custom_call_target="tpu_custom_call" | custom-call | tf_op jit(solution)/shard_map/first_step/pallas_call | solution.py:739
  204.5 7.5 %second_factor.1 = (f32[2,256,256]{2,1,0:T(8,128)}, f32[256,256]{1,0:T(8,128)}, f32[256,256]{1,0:T(8,128)}) custom-call(f32[512,256]{1,0:T(8,128)} %get-tuple-element.26.gram.gram1), custom_call_target="tpu_custom_call" | custom-call | tf_op jit(solution)/shard_map/second_factor/pallas_call | solution.py:778
  212.0 88.4 %second_step.1 = (f32[768,256]{1,0:T(8,128)}, f32[768,256]{1,0:T(8,128)}) custom-call(s32[1,2]{1,0:T(1,128)} %refs_0_.3, s32[1,8]{1,0:T(1,128)} %refs_1_.3, s32[1,49]{1,0:T(1,128)} %get-tuple-element.23.refs_2_, f32[768,256]{1,0:T(8,128)} %get-tuple-element.28.refs_3_, f32[256,256]{1,0:T(8,128)} %get-tuple-element.29.refs_4_, ...), custom_call_target="tpu_custom_call" | custom-call | tf_op jit(solution)/shard_map/second_step/pallas_call | solution.py:739
  300.4 10.2 %last.1 = f32[768,256]{1,0:T(8,128)} custom-call(f32[256,256]{1,0:T(8,128)} %get-tuple-element.21.g0, f32[1,256,256]{2,1,0:T(8,128)} %get-tuple-element.22.m0, f32[512,256]{1,0:T(8,128)} %get-tuple-element.26.gram.gram1, f32[2,256,256]{2,1,0:T(8,128)} %get-tuple-element.27.mn, f32[768,256]{1,0:T(8,128)} %get-tuple-element.34.gram2, ...), custom_call_target="tpu_custom_call" | custom-call | tf_op jit(solution)/shard_map/last/pallas_call | solution.py:787
